TPU v7x, 32 devices: a whole 2x2x4 slice. The times are simulated.
32 devices in a mesh: groups: 2 (over y), expert: 4 (over z), replica: 4 (over x, core).
Axes of the slice: x: 2, y: 2, z: 4, core: 2. Of those that a mesh axis runs over, the one named last changes fastest.
Arguments:
- tokens: bfloat16 [1024, 1024], P(('groups', 'expert')), parts along dimension 0, may hold values from -6 to 6
- out_grad: bfloat16 [1024, 1024], P(('groups', 'expert')), parts along dimension 0, may hold values from -6 to 6
- route_probs: float32 [1024, 6], P(('groups', 'expert')), parts along dimension 0, may hold values from 0.05 to 0.5
- routes: int32 [1024, 6], P(('groups', 'expert')), parts along dimension 0, may hold values from 0 to 63, all different within a row; in each aligned block of 128 rows (0 to 127, 128 to 255, ...) at most 16 rows name the same one
- placement: int32 [64], replicated, may hold values from 0 to 63, each once
- gate_weight: bfloat16 [64, 1024, 1408], P('expert', None, 'replica'), may hold values from -0.1875 to 0.1875
- up_weight: bfloat16 [64, 1024, 1408], P('expert', None, 'replica'), may hold values from -0.1875 to 0.1875
- down_weight: bfloat16 [64, 1408, 1024], P('expert', 'replica'), may hold values from -0.15625 to 0.15625
Outputs:
- layer_out: bfloat16 [1024, 1024], P(('groups', 'expert')), parts along dimension 0
- token_grad: bfloat16 [1024, 1024], P(('groups', 'expert')), parts along dimension 0
- prob_grad: float32 [1024, 6], P(('groups', 'expert')), parts along dimension 0
- gate_grad: bfloat16 [128, 1024, 1408], P(('groups', 'expert'), None, 'replica'), parts along dimension 0
- up_grad: bfloat16 [128, 1024, 1408], P(('groups', 'expert'), None, 'replica'), parts along dimension 0
- down_grad: bfloat16 [128, 1408, 1024], P(('groups', 'expert'), 'replica'), parts along dimension 0
There are 2 independent parts, one for each index of `groups`. A program takes and returns all parts, laid end to end along the dimension named above; an argument that names none is the same for every part. Nothing has to cross between parts.
Inputs may be any that keep to these rules, and one draw needn't show every extreme that they name: `routes`: each row names 6 different experts. In the rows of one device (aligned blocks of 128 rows) no expert is named by more than 16 rows, and in some blocks one expert is named by exactly 16 rows. A permutation: expert e's weights are those of slot placement[e].
All inputs are finite; a program needn't handle non-finite values.
Results may differ from a plain program's by a relative error of at most 0.012.
Values may be sent and summed in bfloat16 or wider, within the bound.
A program may use at most 192 MiB of HBM per device.

v0:
```python
import jax
import jax.numpy as jnp
from jax import lax
from jax.sharding import PartitionSpec as P

MOST = 16


def expert_rows(input_rows, back_rows, gate_weight, up_weight, down_weight):
    gate_pre = jnp.einsum(
        "slcd,ldh->slch", input_rows, gate_weight, preferred_element_type=jnp.float32
    )
    up_pre = jnp.einsum("slcd,ldh->slch", input_rows, up_weight, preferred_element_type=jnp.float32)
    sigma_gate = jax.nn.sigmoid(gate_pre)
    swish_gate = gate_pre * sigma_gate
    hidden = (swish_gate * up_pre).astype(jnp.bfloat16)
    outputs = jnp.einsum("slch,lhd->slcd", hidden, down_weight, preferred_element_type=jnp.float32)
    hidden_grad = jnp.einsum(
        "slcd,lhd->slch", back_rows, down_weight, preferred_element_type=jnp.float32
    )
    gate_back = (hidden_grad * up_pre * sigma_gate * (1.0 + gate_pre * (1.0 - sigma_gate))).astype(
        jnp.bfloat16
    )
    up_back = (hidden_grad * swish_gate).astype(jnp.bfloat16)
    input_grad = jnp.einsum(
        "slch,ldh->slcd", gate_back, gate_weight, preferred_element_type=jnp.float32
    )
    input_grad = input_grad + jnp.einsum(
        "slch,ldh->slcd", up_back, up_weight, preferred_element_type=jnp.float32
    )
    return (outputs, input_grad, hidden, gate_back, up_back)


def shards(tokens, out_grad, route_probs, routes, placement, gate_weight, up_weight, down_weight):
    local_experts = gate_weight.shape[0]
    index_count = lax.axis_size("expert")
    experts_all = placement.shape[0]
    tok_rows, top_k = routes.shape
    model_width = tokens.shape[1]
    capacity = MOST
    expert_ids = jnp.arange(experts_all, dtype=jnp.int32)
    match_table = routes.reshape(-1)[:, None] == expert_ids[None, :]
    slot_ids = jnp.sum(jnp.where(match_table, placement[None, :], 0), axis=1, dtype=jnp.int32)
    slot_match = (slot_ids[:, None] == expert_ids[None, :]).astype(jnp.int32)
    rank_ids = jnp.sum(
        (jnp.cumsum(slot_match, axis=0, dtype=jnp.int32) - 1) * slot_match, axis=1, dtype=jnp.int32
    )
    position = slot_ids * capacity + rank_ids
    route_count = tok_rows * top_k
    buffer_rows = experts_all * capacity
    route_of = (
        jnp.full((buffer_rows,), route_count, jnp.int32)
        .at[position]
        .set(jnp.arange(route_count, dtype=jnp.int32))
    )
    filled = route_of < route_count
    safe_route = jnp.where(filled, route_of, 0)
    token_of = safe_route // top_k
    probs_flat = route_probs.reshape(-1)
    input_send = jnp.where(filled[:, None], tokens[token_of], jnp.zeros((), jnp.bfloat16))
    scaled = probs_flat[safe_route][:, None] * out_grad[token_of].astype(jnp.float32)
    back_send = jnp.where(filled[:, None], scaled, 0.0).astype(jnp.bfloat16)
    buffer_shape = (index_count, local_experts, capacity, model_width)
    input_send = input_send.reshape(buffer_shape)
    back_send = back_send.reshape(buffer_shape)
    input_piece = lax.all_to_all(input_send, "expert", split_axis=0, concat_axis=0, tiled=True)
    back_piece = lax.all_to_all(back_send, "expert", split_axis=0, concat_axis=0, tiled=True)
    results = expert_rows(input_piece, back_piece, gate_weight, up_weight, down_weight)
    input_rows, back_rows, outputs, input_grad, hidden, gate_back, up_back = (
        input_piece,
        back_piece,
    ) + results
    gate_grad = jnp.einsum(
        "slcd,slch->ldh", input_rows, gate_back, preferred_element_type=jnp.float32
    ).astype(jnp.bfloat16)
    up_grad = jnp.einsum(
        "slcd,slch->ldh", input_rows, up_back, preferred_element_type=jnp.float32
    ).astype(jnp.bfloat16)
    down_grad = jnp.einsum(
        "slch,slcd->lhd", hidden, back_rows, preferred_element_type=jnp.float32
    ).astype(jnp.bfloat16)
    out_back, grad_back = (
        lax.all_to_all(
            outputs.astype(jnp.bfloat16), "expert", split_axis=0, concat_axis=0, tiled=True
        ),
        lax.all_to_all(
            input_grad.astype(jnp.bfloat16), "expert", split_axis=0, concat_axis=0, tiled=True
        ),
    )
    kept_mask = rank_ids >= 0
    out_rows = out_back.reshape(-1, model_width)[position].astype(jnp.float32)
    grad_rows = grad_back.reshape(-1, model_width)[position].astype(jnp.float32)
    kept_rows = kept_mask.reshape(tok_rows, top_k)
    route_weight = jnp.where(kept_mask, probs_flat, 0.0).reshape(tok_rows, top_k)
    out_rows = out_rows.reshape(tok_rows, top_k, model_width)
    grad_rows = grad_rows.reshape(tok_rows, top_k, model_width)
    layer_part = jnp.sum(route_weight[:, :, None] * out_rows, axis=1)
    token_part = jnp.sum(jnp.where(kept_rows[:, :, None], grad_rows, 0.0), axis=1)
    prob_part = jnp.where(
        kept_rows, jnp.sum(out_grad.astype(jnp.float32)[:, None, :] * out_rows, axis=2), 0.0
    )
    layer_sum, token_sum, prob_sum = (
        lax.psum(layer_part.astype(jnp.bfloat16), "replica").astype(jnp.float32),
        lax.psum(token_part.astype(jnp.bfloat16), "replica").astype(jnp.float32),
        lax.psum(prob_part.astype(jnp.bfloat16), "replica").astype(jnp.float32),
    )
    return (
        layer_sum.astype(jnp.bfloat16),
        token_sum.astype(jnp.bfloat16),
        prob_sum,
        gate_grad,
        up_grad,
        down_grad,
    )


def solution(mesh):
    in_specs = (
        P(("groups", "expert"), None),
        P(("groups", "expert"), None),
        P(("groups", "expert"), None),
        P(("groups", "expert"), None),
        P(),
        P("expert", None, "replica"),
        P("expert", None, "replica"),
        P("expert", "replica", None),
    )
    out_specs = (
        P(("groups", "expert"), None),
        P(("groups", "expert"), None),
        P(("groups", "expert"), None),
        P(("groups", "expert"), None, "replica"),
        P(("groups", "expert"), None, "replica"),
        P(("groups", "expert"), "replica", None),
    )
    return jax.shard_map(shards, mesh=mesh, in_specs=in_specs, out_specs=out_specs, check_vma=False)
```

profile of v0, /device:TPU:0, one launch (start us, length us, event | category | flops | bytes accessed | tf_op | source)
XLA Modules:
  0.0 306.9 jit_solution(7315500077147831765)
XLA Ops:
  14.7 4.1 %gather_fusion = bf16[1024,1024]{1,0:T(8,128)(2,1)S(1)} fusion(bf16[128,1024]{1,0:T(8,128)(2,1)S(1)} %copy-done, s32[1024]{0:T(1024)S(1)} %get-tuple-element.26), kind=kCustom, calls=%fused_computation | custom fusion | bytes 4198400 | tf_op jit(solution)/shard_map/gather | solution.py:60
  20.4 6.4 %all-to-all-start = ((bf16[4,16,16,1024]{3,2,1,0:T(8,128)(2,1)}), bf16[4,16,16,1024]{3,2,1,0:T(8,128)(2,1)S(1)}, u32[]{:S(2)}, u32[]{:S(2)}) async-start(bf16[4,16,16,1024]{3,2,1,0:T(8,128)(2,1)} %broadcast_select_fusion), calls=%async_computation | async-start | bytes 4194304 | tf_op jit(solution)/shard_map/all_to_all | solution.py:66
  27.1 4.5 %gather_fusion.2 = f32[1024]{0:T(1024)S(1)} fusion(f32[768]{0:T(1024)S(1)} %reshape.123, s32[1024]{0:T(1024)S(1)} %get-tuple-element.25), kind=kCustom, calls=%fused_computation.2 | custom fusion | bytes 12288 | tf_op jit(solution)/shard_map/gather | solution.py:61
  31.7 5.3 %gather_fusion.3 = bf16[1024,1024]{1,0:T(8,128)(2,1)} fusion(bf16[128,1024]{1,0:T(8,128)(2,1)S(1)} %copy-done.2, s32[1024]{0:T(1024)S(1)} %get-tuple-element.26), kind=kCustom, calls=%fused_computation.3 | custom fusion | bytes 4198400 | tf_op jit(solution)/shard_map/gather | solution.py:61
  40.5 34.5 %all-to-all-done = bf16[4,16,16,1024]{3,2,1,0:T(8,128)(2,1)S(1)} async-done(((bf16[4,16,16,1024]{3,2,1,0:T(8,128)(2,1)}), bf16[4,16,16,1024]{3,2,1,0:T(8,128)(2,1)S(1)}, u32[]{:S(2)}, u32[]{:S(2)}) %all-to-all-start) | async-done | bytes 2097184 | tf_op jit(solution)/shard_map/all_to_all | solution.py:66
  75.0 4.6 %all-to-all-start.2 = ((bf16[4,16,16,1024]{3,2,1,0:T(8,128)(2,1)}), bf16[4,16,16,1024]{3,2,1,0:T(8,128)(2,1)}, u32[]{:S(2)}, u32[]{:S(2)}) async-start(bf16[4,16,16,1024]{3,2,1,0:T(8,128)(2,1)} %fusion.13), calls=%async_computation.2 | async-start | bytes 4194304 | tf_op jit(solution)/shard_map/all_to_all | solution.py:67
  79.7 8.7 %fusion.2 = f32[16,4,16,352]{3,2,1,0:T(8,128)} fusion(bf16[16,1024,352]{1,2,0:T(8,128)(2,1)} %param.14, bf16[4,16,16,1024]{3,2,1,0:T(8,128)(2,1)S(1)} %all-to-all-done), kind=kOutput, calls=%fused_computation.11 | convolution fusion | flops 738197504 | bytes 15073280 | tf_op jit(solution)/shard_map/slcd,ldh->slch/dot_general | solution.py:13
  88.4 8.7 %fusion.6 = f32[16,4,16,352]{3,2,1,0:T(8,128)} fusion(bf16[16,1024,352]{1,2,0:T(8,128)(2,1)} %param.13, bf16[4,16,16,1024]{3,2,1,0:T(8,128)(2,1)S(1)} %all-to-all-done), kind=kOutput, calls=%fused_computation.15 | convolution fusion | flops 738197504 | bytes 15073280 | tf_op jit(solution)/shard_map/slcd,ldh->slch/dot_general | solution.py:10
  97.1 30.1 %all-to-all-done.2 = bf16[4,16,16,1024]{3,2,1,0:T(8,128)(2,1)} async-done(((bf16[4,16,16,1024]{3,2,1,0:T(8,128)(2,1)}), bf16[4,16,16,1024]{3,2,1,0:T(8,128)(2,1)}, u32[]{:S(2)}, u32[]{:S(2)}) %all-to-all-start.2) | async-done | bytes 2097184 | tf_op jit(solution)/shard_map/all_to_all | solution.py:67
  127.2 10.0 %fusion.25 = (bf16[4,16,16,352]{3,2,0,1:T(8,128)(2,1)S(1)}, bf16[4,16,16,352]{3,2,0,1:T(8,128)(2,1)S(1)}, bf16[4,16,16,352]{3,2,0,1:T(8,128)(2,1)}) fusion(f32[16,4,16,352]{3,2,1,0:T(8,128)} %fusion.2, f32[16,4,16,352]{3,2,1,0:T(8,128)} %fusion.6, bf16[16,352,1024]{2,1,0:T(8,128)(2,1)} %param.15, bf16[4,16,16,1024]{3,2,1,0:T(8,128)(2,1)} %all-to-all-done.2), kind=kOutput, calls=%fused_computation.39 | convolution fusion | flops 743604224 | bytes 18677760 | tf_op jit(solution)/shard_map/slcd,lhd->slch/dot_general | solution.py:18
  137.2 7.0 %convert_bitcast_fusion = bf16[4,16,16,1024]{3,2,0,1:T(8,128)(2,1)S(1)} fusion(bf16[4,16,16,352]{3,2,0,1:T(8,128)(2,1)S(1)} %get-tuple-element.23, bf16[16,352,1024]{2,1,0:T(8,128)(2,1)} %param.15), kind=kOutput, calls=%fused_computation.29 | convolution fusion | flops 739246080 | bytes 14352384 | tf_op jit(solution)/shard_map/slch,lhd->slcd/dot_general | solution.py:17
  149.5 6.8 %fusion = f32[16,4,16,1024]{3,2,1,0:T(8,128)S(1)} fusion(bf16[4,16,16,352]{3,2,0,1:T(8,128)(2,1)} %get-tuple-element.24, bf16[16,1024,352]{1,2,0:T(8,128)(2,1)} %param.14), kind=kOutput, calls=%fused_computation.9 | convolution fusion | flops 738197504 | bytes 16449536 | tf_op jit(solution)/shard_map/slch,ldh->slcd/dot_general | solution.py:28
  156.4 6.8 %fusion.14 = bf16[4,16,16,1024]{3,2,0,1:T(8,128)(2,1)S(1)} fusion(f32[16,4,16,1024]{3,2,1,0:T(8,128)S(1)} %fusion, bf16[4,16,16,352]{3,2,0,1:T(8,128)(2,1)S(1)} %get-tuple-element.22, bf16[16,1024,352]{1,2,0:T(8,128)(2,1)} %param.13), kind=kOutput, calls=%fused_computation.28 | convolution fusion | flops 740294656 | bytes 18546688 | tf_op jit(solution)/shard_map/slch,ldh->slcd/dot_general | solution.py:25
  164.6 32.4 %all-to-all-done.1 = bf16[4,16,16,1024]{3,2,1,0:T(8,128)(2,1)S(1)} async-done(((bf16[4,16,16,1024]{3,2,1,0:T(8,128)(2,1)}), bf16[4,16,16,1024]{3,2,1,0:T(8,128)(2,1)S(1)}, u32[]{:S(2)}, u32[]{:S(2)}) %all-to-all-start.1) | async-done | bytes 2097184 | tf_op jit(solution)/shard_map/all_to_all | solution.py:83
  196.9 4.4 %all-to-all-start.3 = ((bf16[4,16,16,1024]{3,2,1,0:T(8,128)(2,1)}), bf16[4,16,16,1024]{3,2,1,0:T(8,128)(2,1)}, u32[]{:S(2)}, u32[]{:S(2)}) async-start(bf16[4,16,16,1024]{3,2,1,0:T(8,128)(2,1)} %copy.35), calls=%async_computation.3 | async-start | bytes 4194304 | tf_op jit(solution)/shard_map/all_to_all | solution.py:86
  202.5 9.4 %bitcast_convert_fusion.2 = bf16[16,1024,352]{1,2,0:T(8,128)(2,1)} fusion(bf16[4,16,16,1024]{3,2,1,0:T(8,128)(2,1)} %copy-done.3, bf16[4,16,16,352]{3,2,0,1:T(8,128)(2,1)S(1)} %get-tuple-element.22), kind=kOutput, calls=%fused_computation.8 | convolution fusion | flops 743964672 | bytes 14352384 | tf_op jit(solution)/shard_map/slcd,slch->ldh/dot_general | solution.py:73
  211.9 6.1 %bitcast_convert_fusion.1 = bf16[16,1024,352]{1,2,0:T(8,128)(2,1)} fusion(bf16[4,16,16,1024]{3,2,1,0:T(8,128)(2,1)S(1)} %copy-done.4, bf16[4,16,16,352]{3,2,0,1:T(8,128)(2,1)S(1)} %copy-done.6), kind=kOutput, calls=%fused_computation.7 | convolution fusion | flops 743964672 | bytes 14352384 | tf_op jit(solution)/shard_map/slcd,slch->ldh/dot_general | solution.py:76
  221.6 3.9 %reshape.125 = f32[128,6,1024]{2,1,0:T(8,128)} reshape(bf16[768,1024]{1,0:T(8,128)(2,1)} %gather_fusion.1) | data formatting | bytes 4718592 | tf_op jit(solution)/shard_map/convert_element_type | solution.py:91
  225.5 23.7 %all-to-all-done.3 = bf16[4,16,16,1024]{3,2,1,0:T(8,128)(2,1)} async-done(((bf16[4,16,16,1024]{3,2,1,0:T(8,128)(2,1)}), bf16[4,16,16,1024]{3,2,1,0:T(8,128)(2,1)}, u32[]{:S(2)}, u32[]{:S(2)}) %all-to-all-start.3) | async-done | bytes 2097184 | tf_op jit(solution)/shard_map/all_to_all | solution.py:86
  249.1 5.7 %gather_fusion.4 = bf16[768,1024]{1,0:T(8,128)(2,1)S(1)} fusion(bf16[1024,1024]{1,0:T(8,128)(2,1)} %bitcast.19, s32[1024]{0:T(1024)S(1)} %pad_clamp_fusion), kind=kCustom, calls=%fused_computation.4 | custom fusion | bytes 3148800 | tf_op jit(solution)/shard_map/gather | solution.py:92
  257.0 4.5 %select_reduce_fusion = bf16[128,1024]{1,0:T(8,128)(2,1)} fusion(f32[128,6,1024]{2,1,0:T(8,128)} %reshape.127, pred[128,6]{1,0:T(8,128)(4,1)S(1)} %ge.13), kind=kLoop, calls=%fused_computation.25 | loop fusion | flops 1441792 | bytes 3408640 | tf_op jit(solution)/shard_map/reduce_sum | solution.py:98
  264.2 9.3 %bitcast_convert_fusion = bf16[16,352,1024]{2,1,0:T(8,128)(2,1)} fusion(bf16[4,16,16,352]{3,2,0,1:T(8,128)(2,1)S(1)} %copy-done.9, bf16[4,16,16,1024]{3,2,1,0:T(8,128)(2,1)} %all-to-all-done.2), kind=kOutput, calls=%fused_computation.6 | convolution fusion | flops 743964672 | bytes 14352384 | tf_op jit(solution)/shard_map/slch,slcd->lhd/dot_general | solution.py:79
  273.5 10.5 %psum.23 = bf16[128,6]{1,0:T(8,128)(2,1)S(1)} all-reduce(bf16[128,6]{1,0:T(8,128)(2,1)S(1)} %select_convert_fusion), channel_id=1, replica_groups=mesh['groups'=2,'expert'=4,'replica'=4] {'replica'}, use_global_device_ids=true, to_apply=%region_10.11 | all-reduce | flops 768 | bytes 3072 | tf_op jit(solution)/shard_map/psum | solution.py:105
  284.7 12.1 %all-reduce.3.cloned.1.call-done = (bf16[128,1024]{1,0:T(8,128)(2,1)}, bf16[128,1024]{1,0:T(8,128)(2,1)}) async-done(((bf16[128,1024]{1,0:T(8,128)(2,1)}, bf16[128,1024]{1,0:T(8,128)(2,1)}), (bf16[128,1024]{1,0:T(8,128)(2,1)}, bf16[128,1024]{1,0:T(8,128)(2,1)})) %all-reduce.3.cloned.1.call-update) | async-done | bytes 524304 | tf_op jit(solution)/shard_map/psum | solution.py:103
  (59 shorter events, 33.1 us)
Async XLA Ops:
  7.2 7.6 %copy-start = (bf16[128,1024]{1,0:T(8,128)(2,1)S(1)}, bf16[128,1024]{1,0:T(8,128)(2,1)}, u32[]{:S(2)}) copy-start(bf16[128,1024]{1,0:T(8,128)(2,1)} %param.8) | copy-start | bytes 786436
  20.4 6.5 %copy-start.10 = (f32[128,6]{0,1:T(8,128)S(1)}, f32[128,6]{0,1:T(8,128)}, u32[]{:S(2)}) copy-start(f32[128,6]{0,1:T(8,128)} %param.10) | copy-start | bytes 9220
  20.4 54.6 %all-to-all-start = ((bf16[4,16,16,1024]{3,2,1,0:T(8,128)(2,1)}), bf16[4,16,16,1024]{3,2,1,0:T(8,128)(2,1)S(1)}, u32[]{:S(2)}, u32[]{:S(2)}) async-start(bf16[4,16,16,1024]{3,2,1,0:T(8,128)(2,1)} %broadcast_select_fusion), calls=%async_computation | async-start | bytes 4194304 | tf_op jit(solution)/shard_map/all_to_all | solution.py:66
  27.1 4.6 %copy-start.2 = (bf16[128,1024]{1,0:T(8,128)(2,1)S(1)}, bf16[128,1024]{1,0:T(8,128)(2,1)}, u32[]{:S(2)}) copy-start(bf16[128,1024]{1,0:T(8,128)(2,1)} %param.9) | copy-start | bytes 786436
  75.0 13.4 %copy-start.3 = (bf16[4,16,16,1024]{3,2,1,0:T(8,128)(2,1)}, bf16[4,16,16,1024]{3,2,1,0:T(8,128)(2,1)S(1)}, u32[]{:S(2)}) copy-start(bf16[4,16,16,1024]{3,2,1,0:T(8,128)(2,1)S(1)} %all-to-all-done) | copy-start | bytes 6291460
  75.0 52.2 %all-to-all-start.2 = ((bf16[4,16,16,1024]{3,2,1,0:T(8,128)(2,1)}), bf16[4,16,16,1024]{3,2,1,0:T(8,128)(2,1)}, u32[]{:S(2)}, u32[]{:S(2)}) async-start(bf16[4,16,16,1024]{3,2,1,0:T(8,128)(2,1)} %fusion.13), calls=%async_computation.2 | async-start | bytes 4194304 | tf_op jit(solution)/shard_map/all_to_all | solution.py:67
  137.2 7.0 %copy-start.8 = (bf16[4,16,16,352]{3,2,0,1:T(8,128)(2,1)}, bf16[4,16,16,352]{3,2,0,1:T(8,128)(2,1)S(1)}, u32[]{:S(2)}) copy-start(bf16[4,16,16,352]{3,2,0,1:T(8,128)(2,1)S(1)} %get-tuple-element.23) | copy-start | bytes 2162692
  145.7 51.3 %all-to-all-start.1 = ((bf16[4,16,16,1024]{3,2,1,0:T(8,128)(2,1)}), bf16[4,16,16,1024]{3,2,1,0:T(8,128)(2,1)S(1)}, u32[]{:S(2)}, u32[]{:S(2)}) async-start(bf16[4,16,16,1024]{3,2,1,0:T(8,128)(2,1)} %copy.32), calls=%async_computation.1 | async-start | bytes 4194304 | tf_op jit(solution)/shard_map/all_to_all | solution.py:83
  196.9 52.2 %all-to-all-start.3 = ((bf16[4,16,16,1024]{3,2,1,0:T(8,128)(2,1)}), bf16[4,16,16,1024]{3,2,1,0:T(8,128)(2,1)}, u32[]{:S(2)}, u32[]{:S(2)}) async-start(bf16[4,16,16,1024]{3,2,1,0:T(8,128)(2,1)} %copy.35), calls=%async_computation.3 | async-start | bytes 4194304 | tf_op jit(solution)/shard_map/all_to_all | solution.py:86
  201.4 95.3 %all-reduce.3.cloned.1.call-start = ((), (), s32[]{:S(2)}) async-start(), calls=%async_computation.4 | async-start | bytes 1048576 | tf_op jit(solution)/shard_map/psum | solution.py:103
  202.5 9.4 %copy-start.4 = (bf16[4,16,16,1024]{3,2,1,0:T(8,128)(2,1)S(1)}, bf16[4,16,16,1024]{3,2,1,0:T(8,128)(2,1)}, u32[]{:S(2)}) copy-start(bf16[4,16,16,1024]{3,2,1,0:T(8,128)(2,1)} %copy-done.3) | copy-start | bytes 6291460
  202.5 9.4 %copy-start.6 = (bf16[4,16,16,352]{3,2,0,1:T(8,128)(2,1)S(1)}, bf16[4,16,16,352]{3,2,0,1:T(8,128)(2,1)}, u32[]{:S(2)}) copy-start(bf16[4,16,16,352]{3,2,0,1:T(8,128)(2,1)} %get-tuple-element.24) | copy-start | bytes 2162692
  254.8 6.7 %copy-start.7 = (f32[128,1024]{1,0:T(8,128)S(1)}, f32[128,1024]{1,0:T(8,128)}, u32[]{:S(2)}) copy-start(f32[128,1024]{1,0:T(8,128)} %convert_element_type.100) | copy-start | bytes 1572868
  257.0 4.5 %copy-start.5 = (f32[128,6,1024]{2,1,0:T(8,128)S(1)}, f32[128,6,1024]{2,1,0:T(8,128)}, u32[]{:S(2)}) copy-start(f32[128,6,1024]{2,1,0:T(8,128)} %reshape.125) | copy-start | bytes 9437188
  261.5 2.7 copy-start.9
  264.2 35.8 %copy-start.1 = (bf16[128,1024]{1,0:T(8,128)(2,1)S(1)}, bf16[128,1024]{1,0:T(8,128)(2,1)}, u32[]{:S(2)}) copy-start(bf16[128,1024]{1,0:T(8,128)(2,1)} %param.8) | copy-start | bytes 786436
Sparse Core Ops, SparseCore 0:
  264.3 32.3 all-reduce.2
where the time goes:
time: 308 us; the launch traced here: 307 us
  waiting for transfers between devices  133 us (43%)
  matrix products  72.7 us (24%)
  local copies, waits for them, and re-layouts  41.4 us (13%)
  starting transfers between devices  19.4 us (6%)
  other arithmetic  15.9 us (5%)
  between operations  14.3 us (5%)
  blocking collectives  10.5 us (3%)
    all_to_all x1, waiting for transfers between devices, shards(): lax.all_to_all(input_send, 'expert', split_axis=0, concat_axis=0, tiled=T...  34.5 us
    all_to_all x1, waiting for transfers between devices, shards(): lax.all_to_all(outputs.astype(jnp.bfloat16), 'expert', split_axis=0, conc...  32.4 us
    all_to_all x1, waiting for transfers between devices, shards(): lax.all_to_all(back_send, 'expert', split_axis=0, concat_axis=0, tiled=True)  30.1 us
    all_to_all x1, waiting for transfers between devices, shards(): lax.all_to_all(input_grad.astype(jnp.bfloat16), 'expert', split_axis=0, c...  23.7 us
    psum x1, waiting for transfers between devices, shards(): lax.psum(layer_part.astype(jnp.bfloat16), 'replica').astype(jnp.float32)  12.1 us
    psum x1, blocking collectives, shards(): lax.psum(prob_part.astype(jnp.bfloat16), 'replica').astype(jnp.float32)  10.5 us
    dot_general x1, matrix products, expert_rows(): jnp.einsum('slcd,lhd->slch', back_rows, down_weight, preferred_element_ty...  9.97 us
    dot_general x1, matrix products, shards(): jnp.einsum('slcd,slch->ldh', input_rows, gate_back, preferred_element_typ...  9.36 us
  transfers between devices with their start and end apart: 5, of which 5 were waited for; matrix products, arithmetic and copies ran while one was open for 26% of the time, Pallas kernels for 0%

commit v1 on v0

--- a/solution.py
+++ b/solution.py
@@ -1,9 +1,12 @@
 import jax
 import jax.numpy as jnp
 from jax import lax
+from jax.experimental import pallas as pl
+from jax.experimental.pallas import tpu as pltpu
 from jax.sharding import PartitionSpec as P
 
 MOST = 16
+MESH = pl.DeviceIdType.MESH
 
 
 def expert_rows(input_rows, back_rows, gate_weight, up_weight, down_weight):
@@ -114,6 +117,367 @@
     )
 
 
+def place(expert=None, replica=None):
+    own = [lax.axis_index("groups"), lax.axis_index("expert"), lax.axis_index("replica")]
+    if expert is not None:
+        own[1] = expert
+    if replica is not None:
+        own[2] = replica
+    return tuple(own)
+
+
+def greet(devices):
+    barrier = pltpu.get_barrier_semaphore()
+    for device in devices:
+        pl.semaphore_signal(barrier, inc=1, device_id=device, device_id_type=MESH)
+    pl.semaphore_wait(barrier, len(devices))
+
+
+def positions():
+    e, r = lax.axis_index("expert"), lax.axis_index("replica")
+    core = r + 1 - 2 * lax.rem(r, 2)
+    across = lax.rem(r + 2, 4)
+    diagonal = lax.rem(core + 2, 4)
+    return e, r, core, across, diagonal
+
+
+def remote(src, dst, send, recv, device):
+    copy = pltpu.make_async_remote_copy(
+        src_ref=src, dst_ref=dst, send_sem=send, recv_sem=recv, device_id=device, device_id_type=MESH
+    )
+    copy.start()
+    return copy
+
+
+def gather_kernel(x_ref, g_ref, m_ref, rows_ref, meta_ref, send, recv):
+    e, r, core, across, _ = positions()
+    quarter = x_ref.shape[0] // 4
+    greet(
+        [place(expert=lax.rem(e + j, 4)) for j in (1, 2, 3)]
+        + [place(replica=core), place(replica=across)]
+    )
+    rows_ref[e, 0] = x_ref[...]
+    rows_ref[e, 1] = g_ref[...]
+    meta_ref[e] = m_ref[...]
+    mine = pl.ds(pl.multiple_of(r * quarter, quarter), quarter)
+    other = pl.ds(pl.multiple_of(across * quarter, quarter), quarter)
+    first, metas = {}, {}
+    for j in (2, 1, 3):
+        peer = place(expert=lax.rem(e + j, 4))
+        own = rows_ref.at[e, :, mine]
+        metas[j] = remote(meta_ref.at[e], meta_ref.at[e], send.at[0, j], recv.at[0, j], peer)
+        first[j] = remote(own, own, send.at[1, j], recv.at[1, j], peer)
+    passed, spread, last = {}, {}, {}
+    for j in (1, 3, 2):
+        block = lax.rem(e + 4 - j, 4)
+        first[j].wait_recv()
+        part = rows_ref.at[block, :, mine]
+        passed[j] = remote(part, part, send.at[2, j], recv.at[2, j], place(replica=across))
+        spread[j] = remote(part, part, send.at[3, j], recv.at[3, j], place(replica=core))
+    for j in (1, 3, 2):
+        block = lax.rem(e + 4 - j, 4)
+        passed[j].wait_recv()
+        part = rows_ref.at[block, :, other]
+        last[j] = remote(part, part, send.at[4, j], recv.at[4, j], place(replica=core))
+    for j in (1, 3, 2):
+        metas[j].wait()
+        first[j].wait_send()
+        passed[j].wait_send()
+        spread[j].wait()
+        last[j].wait()
+
+
+def gather_all(tokens, out_grad, meta):
+    block, width = tokens.shape
+    return pl.pallas_call(
+        gather_kernel,
+        out_shape=(
+            jax.ShapeDtypeStruct((4, 2, block, width), jnp.bfloat16),
+            jax.ShapeDtypeStruct((4,) + meta.shape, jnp.float32),
+        ),
+        in_specs=[pl.BlockSpec(memory_space=pltpu.VMEM)] * 3,
+        out_specs=[pl.BlockSpec(memory_space=pltpu.VMEM)] * 2,
+        scratch_shapes=[pltpu.SemaphoreType.DMA((5, 4)), pltpu.SemaphoreType.DMA((5, 4))],
+        compiler_params=pltpu.CompilerParams(
+            collective_id=0, has_side_effects=True, vmem_limit_bytes=24 * 2**20
+        ),
+    )(tokens, out_grad, meta)
+
+
+def dot(left, right, left_dim, right_dim):
+    return lax.dot_general(
+        left, right, (((left_dim,), (right_dim,)), ((), ())), preferred_element_type=jnp.float32
+    )
+
+
+def slot_kernel(
+    rows_ref, meta_ref, gate_ref, up_ref, down_ref,
+    gate_out, up_out, down_out, part_ref, prob_ref,
+    x_rows, g_rows, out_rows, grad_rows, pick_ref, weight_ref, inner_ref,
+):
+    s = pl.program_id(0)
+    slots = pl.num_programs(0)
+    block = rows_ref.shape[2]
+    width = rows_ref.shape[3]
+    top = 6
+    held = slots * MOST
+    base = lax.axis_index("expert") * slots
+
+    def slot_names():
+        names = lax.broadcasted_iota(jnp.int32, (slots, block), 0) + base
+        return names.astype(jnp.float32)
+
+    @pl.when(s == 0)
+    def _():
+        names = slot_names()
+        before = lax.broadcasted_iota(jnp.int32, (block, block), 0)
+        after = lax.broadcasted_iota(jnp.int32, (block, block), 1)
+        earlier = (before < after).astype(jnp.float32).astype(jnp.bfloat16)
+        ranks = lax.broadcasted_iota(jnp.int32, (slots, MOST, block), 1).astype(jnp.float32)
+        for b in range(4):
+            named = jnp.zeros((slots, block), jnp.float32)
+            probs = jnp.zeros((slots, block), jnp.float32)
+            for k in range(top):
+                same = meta_ref[b, k : k + 1, :] == names
+                named = named + jnp.where(same, 1.0, 0.0)
+                probs = probs + jnp.where(same, meta_ref[b, 8 + k : 9 + k, :], 0.0)
+            rank = dot(named.astype(jnp.bfloat16), earlier, 1, 0)
+            rank = jnp.where(named > 0.0, rank, -1.0)
+            pick = jnp.where(rank[:, None, :] == ranks, 1.0, 0.0)
+            weight_ref[:, b] = jnp.sum(pick * probs[:, None, :], axis=2, keepdims=True)
+            chosen = pick.reshape(held, block).astype(jnp.bfloat16)
+            pick_ref[b] = chosen
+            x_rows[:, b] = (
+                dot(chosen, rows_ref[b, 0], 1, 0).astype(jnp.bfloat16).reshape(slots, MOST, width)
+            )
+            g_rows[:, b] = (
+                dot(chosen, rows_ref[b, 1], 1, 0).astype(jnp.bfloat16).reshape(slots, MOST, width)
+            )
+
+    x = x_rows[s].reshape(4 * MOST, width)
+    g = g_rows[s].reshape(4 * MOST, width)
+    weight = weight_ref[s].reshape(4 * MOST, 1)
+    gate_w, up_w, down_w = gate_ref[0], up_ref[0], down_ref[0]
+    gate_pre = dot(x, gate_w, 1, 0)
+    up_pre = dot(x, up_w, 1, 0)
+    plain_grad = dot(g, down_w, 1, 1)
+    sigma = jax.nn.sigmoid(gate_pre)
+    swish = gate_pre * sigma
+    hidden = (swish * up_pre).astype(jnp.bfloat16).astype(jnp.float32)
+    inner = jnp.sum(hidden * plain_grad, axis=1, keepdims=True)
+    inner_ref[s] = inner.reshape(4, MOST, 1)
+    hidden_grad = plain_grad * weight
+    gate_back = (hidden_grad * up_pre * sigma * (1.0 + gate_pre * (1.0 - sigma))).astype(
+        jnp.bfloat16
+    )
+    up_back = (hidden_grad * swish).astype(jnp.bfloat16)
+    scaled = (hidden * weight).astype(jnp.bfloat16)
+    output = dot(scaled, down_w, 1, 0).astype(jnp.bfloat16).reshape(4, MOST, width)
+    input_grad = dot(gate_back, gate_w, 1, 1) + dot(up_back, up_w, 1, 1)
+    input_grad = input_grad.astype(jnp.bfloat16).reshape(4, MOST, width)
+    for b in range(4):
+        out_rows[b, s] = output[b]
+        grad_rows[b, s] = input_grad[b]
+    gate_out[0] = dot(x, gate_back, 0, 0).astype(jnp.bfloat16)
+    up_out[0] = dot(x, up_back, 0, 0).astype(jnp.bfloat16)
+    down_out[0] = dot(scaled, g, 0, 0).astype(jnp.bfloat16)
+
+    @pl.when(s == slots - 1)
+    def _():
+        names = slot_names()
+        quarter = block // 4
+        for b in range(4):
+            chosen = pick_ref[b]
+            for a, held_rows in ((0, out_rows), (1, grad_rows)):
+                total = dot(chosen, held_rows[b].reshape(held, width), 0, 0).astype(jnp.bfloat16)
+                for q in range(4):
+                    part_ref[q, b, a] = total[q * quarter : (q + 1) * quarter]
+            pick = chosen.astype(jnp.float32).reshape(slots, MOST, block)
+            inner_of = jnp.sum(pick * inner_ref[:, b], axis=1)
+            for k in range(top):
+                same = meta_ref[b, k : k + 1, :] == names
+                prob_ref[b, k : k + 1, :] = jnp.sum(
+                    jnp.where(same, inner_of, 0.0), axis=0, keepdims=True
+                )
+            prob_ref[b, top:8, :] = jnp.zeros((8 - top, block), jnp.float32)
+
+
+def slot_pass(rows, meta, gate_weight, up_weight, down_weight):
+    slots, width, units = gate_weight.shape
+    block = rows.shape[2]
+    tall = pl.BlockSpec((1, width, units), lambda s: (s, 0, 0))
+    wide = pl.BlockSpec((1, units, width), lambda s: (s, 0, 0))
+    whole = pl.BlockSpec(memory_space=pltpu.VMEM)
+    row_shape = (slots, 4, MOST, width)
+    back_shape = (4, slots, MOST, width)
+    flops = 2 * 9 * slots * 4 * MOST * width * units
+    return pl.pallas_call(
+        slot_kernel,
+        grid=(slots,),
+        out_shape=(
+            jax.ShapeDtypeStruct((slots, width, units), jnp.bfloat16),
+            jax.ShapeDtypeStruct((slots, width, units), jnp.bfloat16),
+            jax.ShapeDtypeStruct((slots, units, width), jnp.bfloat16),
+            jax.ShapeDtypeStruct((4, 4, 2, block // 4, width), jnp.bfloat16),
+            jax.ShapeDtypeStruct((4, 8, block), jnp.float32),
+        ),
+        in_specs=[whole, whole, tall, tall, wide],
+        out_specs=[tall, tall, wide, whole, whole],
+        scratch_shapes=[
+            pltpu.VMEM(row_shape, jnp.bfloat16),
+            pltpu.VMEM(row_shape, jnp.bfloat16),
+            pltpu.VMEM(back_shape, jnp.bfloat16),
+            pltpu.VMEM(back_shape, jnp.bfloat16),
+            pltpu.VMEM((4, slots * MOST, block), jnp.bfloat16),
+            pltpu.VMEM((slots, 4, MOST, 1), jnp.float32),
+            pltpu.VMEM((slots, 4, MOST, 1), jnp.float32),
+        ],
+        compiler_params=pltpu.CompilerParams(vmem_limit_bytes=48 * 2**20),
+        cost_estimate=pl.CostEstimate(
+            flops=flops, bytes_accessed=12 * slots * width * units, transcendentals=0
+        ),
+    )(rows, meta, gate_weight, up_weight, down_weight)
+
+
+def reduce_kernel(
+    part_ref, prob_ref, layer_ref, token_ref, prob_out,
+    near, crossing, crossed, summed, arrived, final, prob_in, prob_all, send, recv,
+):
+    e, r, core, across, diagonal = positions()
+    quarter = part_ref.shape[3]
+    greet(
+        [place(expert=lax.rem(e + j, 4)) for j in (1, 2, 3)]
+        + [place(replica=lax.rem(r + i, 4)) for i in (1, 2, 3)]
+    )
+    order = (2, 1, 3, 0)
+    block = [lax.rem(e + j, 4) for j in range(4)]
+    far, close, cross, along, back, forth, last = {}, {}, {}, {}, {}, {}, {}
+    for j in order:
+        far[j] = remote(
+            part_ref.at[diagonal, block[j]], near.at[0, j], send.at[0, j], recv.at[0, j],
+            place(replica=core),
+        )
+    for j in (1, 2, 3):
+        back[j] = remote(
+            prob_ref.at[block[j]], prob_in.at[j], send.at[1, j], recv.at[1, j],
+            place(expert=block[j]),
+        )
+    for j in order:
+        close[j] = remote(
+            part_ref.at[core, block[j]], near.at[1, j], send.at[2, j], recv.at[2, j],
+            place(replica=core),
+        )
+
+    def wide(value):
+        return value.astype(jnp.float32)
+
+    for j in order:
+        far[j].wait_recv()
+        crossing[j] = (wide(part_ref[across, block[j]]) + wide(near[0, j])).astype(jnp.bfloat16)
+        cross[j] = remote(
+            crossing.at[j], crossed.at[j], send.at[3, j], recv.at[3, j], place(replica=across)
+        )
+    for j in order:
+        close[j].wait_recv()
+        cross[j].wait_recv()
+        total = wide(part_ref[r, block[j]]) + wide(near[1, j]) + wide(crossed[j])
+        summed[j] = total.astype(jnp.bfloat16)
+        if j > 0:
+            along[j] = remote(
+                summed.at[j], arrived.at[j], send.at[4, j], recv.at[4, j], place(expert=block[j])
+            )
+    for j in (1, 2, 3):
+        back[j].wait_recv()
+    prob_all[r] = prob_ref[e] + prob_in[1] + prob_in[2] + prob_in[3]
+    for i in (1, 2, 3):
+        forth[i] = remote(
+            prob_all.at[r], prob_all.at[r], send.at[5, i], recv.at[5, i],
+            place(replica=lax.rem(r + i, 4)),
+        )
+    for j in (1, 2, 3):
+        along[j].wait_recv()
+    final[r] = (
+        wide(summed[0]) + wide(arrived[1]) + wide(arrived[2]) + wide(arrived[3])
+    ).astype(jnp.bfloat16)
+    own = final.at[r]
+    last[0] = remote(own, own, send.at[6, 0], recv.at[6, 0], place(replica=across))
+    last[1] = remote(own, own, send.at[6, 1], recv.at[6, 1], place(replica=core))
+    for i in (1, 2, 3):
+        forth[i].wait()
+    prob_out[...] = prob_all[0] + prob_all[1] + prob_all[2] + prob_all[3]
+    last[0].wait_recv()
+    passed = final.at[across]
+    last[2] = remote(passed, passed, send.at[6, 2], recv.at[6, 2], place(replica=core))
+    last[1].wait_recv()
+    last[2].wait_recv()
+    for q in range(4):
+        layer_ref[q * quarter : (q + 1) * quarter, :] = final[q, 0]
+        token_ref[q * quarter : (q + 1) * quarter, :] = final[q, 1]
+    for j in order:
+        far[j].wait_send()
+        close[j].wait_send()
+        cross[j].wait_send()
+        if j > 0:
+            back[j].wait_send()
+            along[j].wait_send()
+    for i in range(3):
+        last[i].wait_send()
+
+
+def reduce_all(part, prob):
+    quarter, width = part.shape[3:]
+    block = 4 * quarter
+    piece = (4, 2, quarter, width)
+    return pl.pallas_call(
+        reduce_kernel,
+        out_shape=(
+            jax.ShapeDtypeStruct((block, width), jnp.bfloat16),
+            jax.ShapeDtypeStruct((block, width), jnp.bfloat16),
+            jax.ShapeDtypeStruct((8, block), jnp.float32),
+        ),
+        in_specs=[pl.BlockSpec(memory_space=pltpu.VMEM)] * 2,
+        out_specs=[pl.BlockSpec(memory_space=pltpu.VMEM)] * 3,
+        scratch_shapes=[
+            pltpu.VMEM((2,) + piece, jnp.bfloat16),
+            pltpu.VMEM(piece, jnp.bfloat16),
+            pltpu.VMEM(piece, jnp.bfloat16),
+            pltpu.VMEM(piece, jnp.bfloat16),
+            pltpu.VMEM(piece, jnp.bfloat16),
+            pltpu.VMEM(piece, jnp.bfloat16),
+            pltpu.VMEM((4, 8, block), jnp.float32),
+            pltpu.VMEM((4, 8, block), jnp.float32),
+            pltpu.SemaphoreType.DMA((7, 4)),
+            pltpu.SemaphoreType.DMA((7, 4)),
+        ],
+        compiler_params=pltpu.CompilerParams(
+            collective_id=1, has_side_effects=True, vmem_limit_bytes=24 * 2**20
+        ),
+    )(part, prob)
+
+
+def gathered_shards(
+    tokens, out_grad, route_probs, routes, placement, gate_weight, up_weight, down_weight
+):
+    block, top_k = routes.shape
+    expert_ids = jnp.arange(placement.shape[0], dtype=jnp.int32)
+    matches = routes.T[:, :, None] == expert_ids
+    slot_ids = jnp.sum(jnp.where(matches, placement, 0), axis=2, dtype=jnp.int32)
+    fill = ((0, 8 - top_k), (0, 0))
+    meta = jnp.concatenate(
+        [
+            jnp.pad(slot_ids.astype(jnp.float32), fill, constant_values=-1.0),
+            jnp.pad(route_probs.T, fill),
+        ],
+        axis=0,
+    )
+    rows, meta_all = gather_all(tokens, out_grad, meta)
+    gate_grad, up_grad, down_grad, part, prob = slot_pass(
+        rows, meta_all, gate_weight, up_weight, down_weight
+    )
+    layer_out, token_grad, prob_sum = reduce_all(part, prob)
+    return (layer_out, token_grad, prob_sum[:top_k].T, gate_grad, up_grad, down_grad)
+
+
 def solution(mesh):
     in_specs = (
         P(("groups", "expert"), None),
@@ -133,4 +497,6 @@
         P(("groups", "expert"), None, "replica"),
         P(("groups", "expert"), "replica", None),
     )
-    return jax.shard_map(shards, mesh=mesh, in_specs=in_specs, out_specs=out_specs, check_vma=False)
+    small = mesh.shape["expert"] == 4 and mesh.shape["replica"] == 4
+    body = gathered_shards if small else shards
+    return jax.shard_map(body, mesh=mesh, in_specs=in_specs, out_specs=out_specs, check_vma=False)

time: 308 us -> 167 us (0.54)
  waiting for transfers between devices: 133 us -> 0 us
  Pallas kernels: 0 us -> 95.1 us
  matrix products: 72.7 us -> 0 us
  local copies, waits for them, and re-layouts: 41.4 us -> 67.2 us
  starting transfers between devices: 19.4 us -> 0 us
  other arithmetic: 15.9 us -> 1.5 us
  between operations: 14.3 us -> 0.66 us
  blocking collectives: 10.5 us -> 0 us
    all_to_all x4 -> x0, waiting for transfers between devices: 121 us -> none  [the longest x1 34.5 us: shards(): lax.all_to_all(input_send, 'expert', split_axis=0, concat_axis=0, tiled=T...]
    pallas_call x0 -> x3, Pallas kernels: none -> 95.1 us  [the longest x1 39.7 us: slot_pass(): pl.pallas_call(slot_kernel, grid=(slots,), out_shape=(jax.ShapeDtypeStruc...]
    dot_general x9 -> x0, matrix products: 72.7 us -> none  [the longest x1 9.97 us: expert_rows(): jnp.einsum('slcd,lhd->slch', back_rows, down_weight, preferred_element_ty...]
    unnamed x27 -> x10, local copies, waits for them, and re-layouts: 5.02 us -> 66.6 us
    gather x5 -> x0, local copies, waits for them, and re-layouts: 23.2 us -> none  [the longest x1 5.68 us: shards(): grad_rows = grad_back.reshape(-1, model_width)[position].astype(jnp.float32)]
    all_to_all x4 -> x0, starting transfers between devices: 19.3 us -> none  [the longest x1 6.45 us: shards(): lax.all_to_all(input_send, 'expert', split_axis=0, concat_axis=0, tiled=T...]
    psum x1 -> x0, waiting for transfers between devices: 12.1 us -> none  [shards(): lax.psum(layer_part.astype(jnp.bfloat16), 'replica').astype(jnp.float32)]
    psum x1 -> x0, blocking collectives: 10.5 us -> none  [shards(): lax.psum(prob_part.astype(jnp.bfloat16), 'replica').astype(jnp.float32)]
  transfers between devices with their start and end apart: 5 -> 0, of which waited for: 5 -> 0; matrix products, arithmetic and copies ran while one was open for 26% -> 0% of each run, Pallas kernels for 0% -> 0%
where the time goes in v1:
time: 167 us; the launch traced here: 164 us
  Pallas kernels  95.1 us (57%)
  local copies, waits for them, and re-layouts  67.2 us (40%)
    unnamed x10, local copies, waits for them, and re-layouts  66.6 us
    pallas_call x1, Pallas kernels, slot_pass(): pl.pallas_call(slot_kernel, grid=(slots,), out_shape=(jax.ShapeDtypeStruc...  39.7 us
    pallas_call x1, Pallas kernels, reduce_all(): pl.pallas_call(reduce_kernel, out_shape=(jax.ShapeDtypeStruct((block, wid...  31.4 us
    pallas_call x1, Pallas kernels, gather_all(): pl.pallas_call(gather_kernel, out_shape=(jax.ShapeDtypeStruct((4, 2, bloc...  24 us

profile of v1, /device:TPU:0, one launch (start us, length us, event | category | flops | bytes accessed | tf_op | source)
XLA Modules:
  0.0 164.5 jit_solution(17560028298702935302)
XLA Ops:
  0.6 0.8 select_reduce_fusion
  1.4 0.7 select_maximum_fusion.m_ref
  2.1 0.0 copy-start
  2.1 0.9 copy-done
  3.1 0.0 copy-start.1
  3.1 0.9 copy-done.1
  4.0 24.0 %shard_map.127 = (bf16[4,2,128,1024]{3,2,1,0:T(8,128)(2,1)S(1)}, f32[4,16,128]{2,1,0:T(8,128)S(1)}) custom-call(bf16[128,1024]{1,0:T(8,128)(2,1)S(1)} %copy-done, bf16[128,1024]{1,0:T(8,128)(2,1)S(1)} %copy-done.1, f32[16,128]{1,0:T(8,128)S(1)} %select_maximum_fusion.m_ref), custom_call_target="tpu_custom_call" | custom-call | tf_op jit(solution)/shard_map/pallas_call | solution.py:192
  28.1 15.6 %copy.18.gate_ref = bf16[16,1024,352]{2,1,0:T(8,128)(2,1)} copy(bf16[16,1024,352]{1,2,0:T(8,128)(2,1)} %param.13) | data formatting | bytes 23068672 | tf_op args[5]
  43.6 15.3 %copy.19.up_ref = bf16[16,1024,352]{2,1,0:T(8,128)(2,1)} copy(bf16[16,1024,352]{1,2,0:T(8,128)(2,1)} %param.14) | data formatting | bytes 23068672 | tf_op args[6]
  58.9 39.7 %shard_map.128 = (bf16[16,1024,352]{2,1,0:T(8,128)(2,1)}, bf16[16,1024,352]{2,1,0:T(8,128)(2,1)}, bf16[16,352,1024]{2,1,0:T(8,128)(2,1)}, bf16[4,4,2,32,1024]{4,3,2,1,0:T(8,128)(2,1)S(1)}, f32[4,8,128]{2,1,0:T(8,128)S(1)}) custom-call(bf16[4,2,128,1024]{3,2,1,0:T(8,128)(2,1)S(1)} %get-tuple-element.16.rows_ref, ...), custom_call_target="tpu_custom_call" | custom-call | flops 6643777536 | bytes 69206016 | tf_op jit(solution)/shard_map/pallas_call | solution.py:314
  98.6 31.4 %shard_map.129 = (bf16[128,1024]{1,0:T(8,128)(2,1)S(1)}, bf16[128,1024]{1,0:T(8,128)(2,1)S(1)}, f32[8,128]{1,0:T(8,128)S(1)}) custom-call(bf16[4,4,2,32,1024]{4,3,2,1,0:T(8,128)(2,1)S(1)} %get-tuple-element.18.part_ref, f32[4,8,128]{2,1,0:T(8,128)S(1)} %get-tuple-element.19.prob_ref), custom_call_target="tpu_custom_call" | custom-call | tf_op jit(solution)/shard_map/pallas_call | solution.py:431
  130.0 0.6 slice_bitcast_fusion
  130.6 16.2 %copy.20 = bf16[16,1024,352]{1,2,0:T(8,128)(2,1)} copy(bf16[16,1024,352]{2,1,0:T(8,128)(2,1)} %get-tuple-element.35) | data formatting | bytes 23068672
  146.8 16.2 %copy.21 = bf16[16,1024,352]{1,2,0:T(8,128)(2,1)} copy(bf16[16,1024,352]{2,1,0:T(8,128)(2,1)} %get-tuple-element.36) | data formatting | bytes 23068672
  163.1 0.7 copy.24
  163.8 0.7 copy.25
  (1 shorter events, 0.0 us)
Async XLA Ops:
  2.1 0.9 copy-start
  3.1 0.9 copy-start.1

commit v2 on v1

--- a/solution.py
+++ b/solution.py
@@ -258,8 +258,8 @@
     g = g_rows[s].reshape(4 * MOST, width)
     weight = weight_ref[s].reshape(4 * MOST, 1)
     gate_w, up_w, down_w = gate_ref[0], up_ref[0], down_ref[0]
-    gate_pre = dot(x, gate_w, 1, 0)
-    up_pre = dot(x, up_w, 1, 0)
+    gate_pre = dot(x, gate_w, 1, 1)
+    up_pre = dot(x, up_w, 1, 1)
     plain_grad = dot(g, down_w, 1, 1)
     sigma = jax.nn.sigmoid(gate_pre)
     swish = gate_pre * sigma
@@ -273,13 +273,13 @@
     up_back = (hidden_grad * swish).astype(jnp.bfloat16)
     scaled = (hidden * weight).astype(jnp.bfloat16)
     output = dot(scaled, down_w, 1, 0).astype(jnp.bfloat16).reshape(4, MOST, width)
-    input_grad = dot(gate_back, gate_w, 1, 1) + dot(up_back, up_w, 1, 1)
+    input_grad = dot(gate_back, gate_w, 1, 0) + dot(up_back, up_w, 1, 0)
     input_grad = input_grad.astype(jnp.bfloat16).reshape(4, MOST, width)
     for b in range(4):
         out_rows[b, s] = output[b]
         grad_rows[b, s] = input_grad[b]
-    gate_out[0] = dot(x, gate_back, 0, 0).astype(jnp.bfloat16)
-    up_out[0] = dot(x, up_back, 0, 0).astype(jnp.bfloat16)
+    gate_out[0] = dot(gate_back, x, 0, 0).astype(jnp.bfloat16)
+    up_out[0] = dot(up_back, x, 0, 0).astype(jnp.bfloat16)
     down_out[0] = dot(scaled, g, 0, 0).astype(jnp.bfloat16)
 
     @pl.when(s == slots - 1)
@@ -303,9 +303,8 @@
 
 
 def slot_pass(rows, meta, gate_weight, up_weight, down_weight):
-    slots, width, units = gate_weight.shape
+    slots, units, width = gate_weight.shape
     block = rows.shape[2]
-    tall = pl.BlockSpec((1, width, units), lambda s: (s, 0, 0))
     wide = pl.BlockSpec((1, units, width), lambda s: (s, 0, 0))
     whole = pl.BlockSpec(memory_space=pltpu.VMEM)
     row_shape = (slots, 4, MOST, width)
@@ -315,14 +314,14 @@
         slot_kernel,
         grid=(slots,),
         out_shape=(
-            jax.ShapeDtypeStruct((slots, width, units), jnp.bfloat16),
-            jax.ShapeDtypeStruct((slots, width, units), jnp.bfloat16),
+            jax.ShapeDtypeStruct((slots, units, width), jnp.bfloat16),
+            jax.ShapeDtypeStruct((slots, units, width), jnp.bfloat16),
             jax.ShapeDtypeStruct((slots, units, width), jnp.bfloat16),
             jax.ShapeDtypeStruct((4, 4, 2, block // 4, width), jnp.bfloat16),
             jax.ShapeDtypeStruct((4, 8, block), jnp.float32),
         ),
-        in_specs=[whole, whole, tall, tall, wide],
-        out_specs=[tall, tall, wide, whole, whole],
+        in_specs=[whole, whole, wide, wide, wide],
+        out_specs=[wide, wide, wide, whole, whole],
         scratch_shapes=[
             pltpu.VMEM(row_shape, jnp.bfloat16),
             pltpu.VMEM(row_shape, jnp.bfloat16),
@@ -472,8 +471,9 @@
     )
     rows, meta_all = gather_all(tokens, out_grad, meta)
     gate_grad, up_grad, down_grad, part, prob = slot_pass(
-        rows, meta_all, gate_weight, up_weight, down_weight
-    )
+        rows, meta_all, jnp.swapaxes(gate_weight, 1, 2), jnp.swapaxes(up_weight, 1, 2), down_weight
+    )
+    gate_grad, up_grad = jnp.swapaxes(gate_grad, 1, 2), jnp.swapaxes(up_grad, 1, 2)
     layer_out, token_grad, prob_sum = reduce_all(part, prob)
     return (layer_out, token_grad, prob_sum[:top_k].T, gate_grad, up_grad, down_grad)
 

time: 167 us -> 101 us (0.60)
  local copies, waits for them, and re-layouts: 67.2 us -> 3.9 us
    unnamed x10 -> x6, local copies, waits for them, and re-layouts: 66.6 us -> 3.3 us
where the time goes in v2:
time: 101 us; the launch traced here: 99.8 us
  Pallas kernels  93.7 us (93%)
  local copies, waits for them, and re-layouts  3.9 us (4%)
  other arithmetic  1.5 us (1%)
    pallas_call x1, Pallas kernels, slot_pass(): pl.pallas_call(slot_kernel, grid=(slots,), out_shape=(jax.ShapeDtypeStruc...  38.3 us
    pallas_call x1, Pallas kernels, reduce_all(): pl.pallas_call(reduce_kernel, out_shape=(jax.ShapeDtypeStruct((block, wid...  31.4 us
    pallas_call x1, Pallas kernels, gather_all(): pl.pallas_call(gather_kernel, out_shape=(jax.ShapeDtypeStruct((4, 2, bloc...  24 us
    unnamed x6, local copies, waits for them, and re-layouts  3.3 us

profile of v2, /device:TPU:0, one launch (start us, length us, event | category | flops | bytes accessed | tf_op | source)
XLA Modules:
  0.0 99.8 jit_solution(4007955006178359010)
XLA Ops:
  0.6 0.8 select_reduce_fusion
  1.4 0.7 select_maximum_fusion.m_ref
  2.1 0.0 copy-start
  2.1 0.9 copy-done
  3.1 0.0 copy-start.1
  3.1 0.9 copy-done.1
  4.0 24.0 %shard_map.127 = (bf16[4,2,128,1024]{3,2,1,0:T(8,128)(2,1)S(1)}, f32[4,16,128]{2,1,0:T(8,128)S(1)}) custom-call(bf16[128,1024]{1,0:T(8,128)(2,1)S(1)} %copy-done, bf16[128,1024]{1,0:T(8,128)(2,1)S(1)} %copy-done.1, f32[16,128]{1,0:T(8,128)S(1)} %select_maximum_fusion.m_ref), custom_call_target="tpu_custom_call" | custom-call | tf_op jit(solution)/shard_map/pallas_call | solution.py:192
  28.1 38.3 %shard_map.128 = (bf16[16,352,1024]{2,1,0:T(8,128)(2,1)}, bf16[16,352,1024]{2,1,0:T(8,128)(2,1)}, bf16[16,352,1024]{2,1,0:T(8,128)(2,1)}, bf16[4,4,2,32,1024]{4,3,2,1,0:T(8,128)(2,1)S(1)}, f32[4,8,128]{2,1,0:T(8,128)S(1)}) custom-call(bf16[4,2,128,1024]{3,2,1,0:T(8,128)(2,1)S(1)} %get-tuple-element.16.rows_ref, ...), custom_call_target="tpu_custom_call" | custom-call | flops 6643777536 | bytes 69206016 | tf_op jit(solution)/shard_map/pallas_call | solution.py:313
  66.4 31.4 %shard_map.129 = (bf16[128,1024]{1,0:T(8,128)(2,1)S(1)}, bf16[128,1024]{1,0:T(8,128)(2,1)S(1)}, f32[8,128]{1,0:T(8,128)S(1)}) custom-call(bf16[4,4,2,32,1024]{4,3,2,1,0:T(8,128)(2,1)S(1)} %get-tuple-element.18.part_ref, f32[4,8,128]{2,1,0:T(8,128)S(1)} %get-tuple-element.19.prob_ref), custom_call_target="tpu_custom_call" | custom-call | tf_op jit(solution)/shard_map/pallas_call | solution.py:430
  97.8 0.6 slice_bitcast_fusion
  98.4 0.7 copy.16
  99.1 0.7 copy.17
  (1 shorter events, 0.0 us)
Async XLA Ops:
  2.1 0.9 copy-start
  3.1 0.9 copy-start.1

commit v3 on v0

--- a/solution.py
+++ b/solution.py
@@ -1,9 +1,12 @@
 import jax
 import jax.numpy as jnp
 from jax import lax
+from jax.experimental import pallas as pl
+from jax.experimental.pallas import tpu as pltpu
 from jax.sharding import PartitionSpec as P
 
 MOST = 16
+MESH = pl.DeviceIdType.MESH
 
 
 def expert_rows(input_rows, back_rows, gate_weight, up_weight, down_weight):
@@ -114,6 +117,438 @@
     )
 
 
+def place(expert=None, replica=None):
+    own = [lax.axis_index("groups"), lax.axis_index("expert"), lax.axis_index("replica")]
+    if expert is not None:
+        own[1] = expert
+    if replica is not None:
+        own[2] = replica
+    return tuple(own)
+
+
+def greet(devices):
+    barrier = pltpu.get_barrier_semaphore()
+    for device in devices:
+        pl.semaphore_signal(barrier, inc=1, device_id=device, device_id_type=MESH)
+    pl.semaphore_wait(barrier, len(devices))
+
+
+def positions():
+    e, r = lax.axis_index("expert"), lax.axis_index("replica")
+    core = r + 1 - 2 * lax.rem(r, 2)
+    across = lax.rem(r + 2, 4)
+    diagonal = lax.rem(core + 2, 4)
+    return e, r, core, across, diagonal
+
+
+def remote(src, dst, send, recv, device):
+    copy = pltpu.make_async_remote_copy(
+        src_ref=src, dst_ref=dst, send_sem=send, recv_sem=recv, device_id=device, device_id_type=MESH
+    )
+    copy.start()
+    return copy
+
+
+def dot(left, right, left_dim, right_dim):
+    return lax.dot_general(
+        left, right, (((left_dim,), (right_dim,)), ((), ())), preferred_element_type=jnp.float32
+    )
+
+def route_kernel(
+    x_ref, g_ref, m_ref, gate_hbm, up_hbm, down_hbm,
+    layer_ref, token_ref, prob_out, x_rows, g_rows, scaled_ref, gate_back_ref, up_back_ref,
+    rows_ref, meta_ref, gate_ref, up_ref, down_ref, gate_pre_ref, up_pre_ref, back_rows,
+    pick_ref, weight_ref, inner_ref, part_ref, near, crossing, crossed, summed, arrived, final,
+    prob_ref, prob_in, prob_all, load, send, recv, add_send, add_recv, prob_send, prob_recv,
+):
+    e, r, core, across, diagonal = positions()
+    slots, units, width = gate_ref.shape
+    block = x_ref.shape[0]
+    quarter = block // 4
+    top = 6
+    held = slots * MOST
+    rows = 4 * MOST
+    mine = pl.ds(pl.multiple_of(r * quarter, quarter), quarter)
+    other = pl.ds(pl.multiple_of(across * quarter, quarter), quarter)
+    weights = ((gate_hbm, gate_ref), (up_hbm, up_ref), (down_hbm, down_ref))
+
+    def fetch(s, start):
+        for i, (source, target) in enumerate(weights):
+            copy = pltpu.make_async_copy(source.at[s], target.at[s], load.at[i, s])
+            if start:
+                copy.start()
+            else:
+                copy.wait()
+
+    def start_fetch(s, carry):
+        fetch(s, True)
+        return carry
+
+    lax.fori_loop(0, slots, start_fetch, 0)
+    rows_ref[0, e] = x_ref[...]
+    rows_ref[1, e] = g_ref[...]
+    meta_ref[e] = m_ref[...]
+    greet(
+        [place(expert=lax.rem(e + j, 4)) for j in (1, 2, 3)]
+        + [place(replica=lax.rem(r + i, 4)) for i in (1, 2, 3)]
+    )
+    metas, first, passed, spread, last = {}, {}, {}, {}, {}
+    for j in (2, 1, 3):
+        peer = place(expert=lax.rem(e + j, 4))
+        metas[j] = remote(meta_ref.at[e], meta_ref.at[e], send.at[0, 0, j], recv.at[0, 0, j], peer)
+    for a in (0, 1):
+        for j in (2, 1, 3):
+            peer = place(expert=lax.rem(e + j, 4))
+            own = rows_ref.at[a, e, mine]
+            first[a, j] = remote(own, own, send.at[a, 1, j], recv.at[a, 1, j], peer)
+
+    def pass_on(a):
+        for j in (1, 3, 2):
+            first[a, j].wait_recv()
+            part = rows_ref.at[a, lax.rem(e + 4 - j, 4), mine]
+            passed[a, j] = remote(
+                part, part, send.at[a, 2, j], recv.at[a, 2, j], place(replica=across)
+            )
+            spread[a, j] = remote(
+                part, part, send.at[a, 3, j], recv.at[a, 3, j], place(replica=core)
+            )
+
+    def pass_last(a):
+        for j in (1, 3, 2):
+            passed[a, j].wait_recv()
+            part = rows_ref.at[a, lax.rem(e + 4 - j, 4), other]
+            last[a, j] = remote(part, part, send.at[a, 4, j], recv.at[a, 4, j], place(replica=core))
+
+    def received(a):
+        for j in (1, 3, 2):
+            spread[a, j].wait_recv()
+            last[a, j].wait_recv()
+
+    def slot_names():
+        names = lax.broadcasted_iota(jnp.int32, (slots, block), 0) + e * slots
+        return names.astype(jnp.float32)
+
+    def wide(value):
+        return value.astype(jnp.float32)
+
+    def choose():
+        names = slot_names()
+        before = lax.broadcasted_iota(jnp.int32, (block, block), 0)
+        after = lax.broadcasted_iota(jnp.int32, (block, block), 1)
+        earlier = (before < after).astype(jnp.float32).astype(jnp.bfloat16)
+        ranks = lax.broadcasted_iota(jnp.int32, (slots, MOST, block), 1).astype(jnp.float32)
+        for b in range(4):
+            named = jnp.zeros((slots, block), jnp.float32)
+            probs = jnp.zeros((slots, block), jnp.float32)
+            for k in range(top):
+                same = meta_ref[b, k : k + 1, :] == names
+                named = named + jnp.where(same, 1.0, 0.0)
+                probs = probs + jnp.where(same, meta_ref[b, 8 + k : 9 + k, :], 0.0)
+            rank = dot(named.astype(jnp.bfloat16), earlier, 1, 0)
+            rank = jnp.where(named > 0.0, rank, -1.0)
+            pick = jnp.where(rank[:, None, :] == ranks, 1.0, 0.0)
+            weight_ref[:, b] = jnp.sum(pick * probs[:, None, :], axis=2, keepdims=True)
+            pick_ref[b] = pick.reshape(held, block).astype(jnp.bfloat16)
+
+    def take(a, target):
+        for b in range(4):
+            target[:, b] = (
+                dot(pick_ref[b], rows_ref[a, b], 1, 0)
+                .astype(jnp.bfloat16)
+                .reshape(slots, MOST, width)
+            )
+
+    def keep(s, value):
+        value = value.astype(jnp.bfloat16).reshape(4, MOST, width)
+        for b in range(4):
+            back_rows[b, s] = value[b]
+
+    def forward(s, carry):
+        fetch(s, False)
+        x = x_rows[s].reshape(rows, width)
+        gate_pre = dot(x, gate_ref[s], 1, 1)
+        up_pre = dot(x, up_ref[s], 1, 1)
+        gate_pre_ref[s] = gate_pre
+        up_pre_ref[s] = up_pre
+        hidden = wide((gate_pre * jax.nn.sigmoid(gate_pre) * up_pre).astype(jnp.bfloat16))
+        scaled = (hidden * weight_ref[s].reshape(rows, 1)).astype(jnp.bfloat16)
+        scaled_ref[s] = scaled
+        keep(s, dot(scaled, down_ref[s], 1, 0))
+        return carry
+
+    def backward(s, carry):
+        g = g_rows[s].reshape(rows, width)
+        gate_pre, up_pre = gate_pre_ref[s], up_pre_ref[s]
+        plain_grad = dot(g, down_ref[s], 1, 1)
+        sigma = jax.nn.sigmoid(gate_pre)
+        swish = gate_pre * sigma
+        hidden = wide((swish * up_pre).astype(jnp.bfloat16))
+        inner = jnp.sum(hidden * plain_grad, axis=1, keepdims=True)
+        inner_ref[s] = inner.reshape(4, MOST, 1)
+        hidden_grad = plain_grad * weight_ref[s].reshape(rows, 1)
+        gate_back = (hidden_grad * up_pre * sigma * (1.0 + gate_pre * (1.0 - sigma))).astype(
+            jnp.bfloat16
+        )
+        up_back = (hidden_grad * swish).astype(jnp.bfloat16)
+        gate_back_ref[s] = gate_back
+        up_back_ref[s] = up_back
+        keep(s, dot(gate_back, gate_ref[s], 1, 0) + dot(up_back, up_ref[s], 1, 0))
+        return carry
+
+    order = (2, 1, 3, 0)
+    where = [lax.rem(e + j, 4) for j in range(4)]
+    far, close, cross, along, end = {}, {}, {}, {}, {}
+
+    def gather_back(a):
+        for j in order:
+            total = dot(pick_ref[where[j]], back_rows[where[j]].reshape(held, width), 0, 0)
+            total = total.astype(jnp.bfloat16)
+            for q in range(4):
+                part_ref[a, q, j] = total[q * quarter : (q + 1) * quarter]
+            far[a, j] = remote(
+                part_ref.at[a, diagonal, j], near.at[a, 0, j], add_send.at[a, 0, j],
+                add_recv.at[a, 0, j], place(replica=core),
+            )
+            close[a, j] = remote(
+                part_ref.at[a, core, j], near.at[a, 1, j], add_send.at[a, 1, j],
+                add_recv.at[a, 1, j], place(replica=core),
+            )
+
+    def add_near(a):
+        for j in order:
+            far[a, j].wait_recv()
+            total = wide(part_ref[a, across, j]) + wide(near[a, 0, j])
+            crossing[a, j] = total.astype(jnp.bfloat16)
+            cross[a, j] = remote(
+                crossing.at[a, j], crossed.at[a, j], add_send.at[a, 2, j], add_recv.at[a, 2, j],
+                place(replica=across),
+            )
+
+    def add_crossed(a):
+        for j in order:
+            close[a, j].wait_recv()
+            cross[a, j].wait_recv()
+            total = wide(part_ref[a, r, j]) + wide(near[a, 1, j]) + wide(crossed[a, j])
+            summed[a, j] = total.astype(jnp.bfloat16)
+            if j > 0:
+                along[a, j] = remote(
+                    summed.at[a, j], arrived.at[a, j], add_send.at[a, 3, j], add_recv.at[a, 3, j],
+                    place(expert=where[j]),
+                )
+
+    def add_along(a):
+        for j in (1, 2, 3):
+            along[a, j].wait_recv()
+        total = wide(summed[a, 0]) + wide(arrived[a, 1])
+        total = total + wide(arrived[a, 2]) + wide(arrived[a, 3])
+        final[a, r] = total.astype(jnp.bfloat16)
+        own = final.at[a, r]
+        end[a, 0] = remote(
+            own, own, add_send.at[a, 4, 0], add_recv.at[a, 4, 0], place(replica=across)
+        )
+        end[a, 1] = remote(
+            own, own, add_send.at[a, 4, 1], add_recv.at[a, 4, 1], place(replica=core)
+        )
+
+    def hand_on(a):
+        end[a, 0].wait_recv()
+        got = final.at[a, across]
+        end[a, 2] = remote(
+            got, got, add_send.at[a, 4, 2], add_recv.at[a, 4, 2], place(replica=core)
+        )
+
+    def finish(a, target):
+        end[a, 1].wait_recv()
+        end[a, 2].wait_recv()
+        for q in range(4):
+            target[q * quarter : (q + 1) * quarter, :] = final[a, q]
+
+    for j in (1, 2, 3):
+        metas[j].wait_recv()
+    choose()
+    pass_on(0)
+    pass_last(0)
+    pass_on(1)
+    received(0)
+    take(0, x_rows)
+    some = slots // 4
+    lax.fori_loop(0, some, forward, 0)
+    pass_last(1)
+    lax.fori_loop(some, slots, forward, 0)
+    gather_back(0)
+    received(1)
+    take(1, g_rows)
+    add_near(0)
+    lax.fori_loop(0, slots // 2, backward, 0)
+    add_crossed(0)
+    lax.fori_loop(slots // 2, slots, backward, 0)
+    gather_back(1)
+    back, forth = {}, {}
+    names = slot_names()
+    for b in range(4):
+        pick = wide(pick_ref[b]).reshape(slots, MOST, block)
+        inner_of = jnp.sum(pick * inner_ref[:, b], axis=1)
+        for k in range(top):
+            same = meta_ref[b, k : k + 1, :] == names
+            prob_ref[b, k : k + 1, :] = jnp.sum(
+                jnp.where(same, inner_of, 0.0), axis=0, keepdims=True
+            )
+        prob_ref[b, top:8, :] = jnp.zeros((8 - top, block), jnp.float32)
+    for j in (1, 2, 3):
+        back[j] = remote(
+            prob_ref.at[where[j]], prob_in.at[j], prob_send.at[0, j], prob_recv.at[0, j],
+            place(expert=where[j]),
+        )
+    add_near(1)
+    add_along(0)
+    hand_on(0)
+    add_crossed(1)
+    for j in (1, 2, 3):
+        back[j].wait_recv()
+    prob_all[r] = prob_ref[e] + prob_in[1] + prob_in[2] + prob_in[3]
+    for i in (1, 2, 3):
+        forth[i] = remote(
+            prob_all.at[r], prob_all.at[r], prob_send.at[1, i], prob_recv.at[1, i],
+            place(replica=lax.rem(r + i, 4)),
+        )
+    finish(0, layer_ref)
+    add_along(1)
+    for i in (1, 2, 3):
+        forth[i].wait()
+    prob_out[...] = prob_all[0] + prob_all[1] + prob_all[2] + prob_all[3]
+    hand_on(1)
+    finish(1, token_ref)
+    for j in (1, 2, 3):
+        metas[j].wait_send()
+        back[j].wait_send()
+    for a in (0, 1):
+        for j in (1, 2, 3):
+            first[a, j].wait_send()
+            passed[a, j].wait_send()
+            spread[a, j].wait_send()
+            last[a, j].wait_send()
+            along[a, j].wait_send()
+        for j in order:
+            far[a, j].wait_send()
+            close[a, j].wait_send()
+            cross[a, j].wait_send()
+        for i in range(3):
+            end[a, i].wait_send()
+
+
+def route_pass(tokens, out_grad, meta, gate_weight, up_weight, down_weight):
+    slots, units, width = gate_weight.shape
+    block = tokens.shape[0]
+    rows = 4 * MOST
+    half = jnp.bfloat16
+    piece = (4, block // 4, width)
+    whole = pl.BlockSpec(memory_space=pltpu.VMEM)
+    left = pl.BlockSpec(memory_space=pl.ANY)
+    return pl.pallas_call(
+        route_kernel,
+        out_shape=(
+            jax.ShapeDtypeStruct((block, width), half),
+            jax.ShapeDtypeStruct((block, width), half),
+            jax.ShapeDtypeStruct((8, block), jnp.float32),
+            jax.ShapeDtypeStruct((slots, 4, MOST, width), half),
+            jax.ShapeDtypeStruct((slots, 4, MOST, width), half),
+            jax.ShapeDtypeStruct((slots, rows, units), half),
+            jax.ShapeDtypeStruct((slots, rows, units), half),
+            jax.ShapeDtypeStruct((slots, rows, units), half),
+        ),
+        in_specs=[whole, whole, whole, left, left, left],
+        out_specs=[whole] * 8,
+        scratch_shapes=[
+            pltpu.VMEM((2, 4, block, width), half),
+            pltpu.VMEM((4,) + meta.shape, jnp.float32),
+            pltpu.VMEM((slots, units, width), half),
+            pltpu.VMEM((slots, units, width), half),
+            pltpu.VMEM((slots, units, width), half),
+            pltpu.VMEM((slots, rows, units), jnp.float32),
+            pltpu.VMEM((slots, rows, units), jnp.float32),
+            pltpu.VMEM((4, slots, MOST, width), half),
+            pltpu.VMEM((4, slots * MOST, block), half),
+            pltpu.VMEM((slots, 4, MOST, 1), jnp.float32),
+            pltpu.VMEM((slots, 4, MOST, 1), jnp.float32),
+            pltpu.VMEM((2, 4) + piece, half),
+            pltpu.VMEM((2, 2) + piece, half),
+            pltpu.VMEM((2,) + piece, half),
+            pltpu.VMEM((2,) + piece, half),
+            pltpu.VMEM((2,) + piece, half),
+            pltpu.VMEM((2,) + piece, half),
+            pltpu.VMEM((2,) + piece, half),
+            pltpu.VMEM((4, 8, block), jnp.float32),
+            pltpu.VMEM((4, 8, block), jnp.float32),
+            pltpu.VMEM((4, 8, block), jnp.float32),
+            pltpu.SemaphoreType.DMA((3, slots)),
+            pltpu.SemaphoreType.DMA((2, 5, 4)),
+            pltpu.SemaphoreType.DMA((2, 5, 4)),
+            pltpu.SemaphoreType.DMA((2, 5, 4)),
+            pltpu.SemaphoreType.DMA((2, 5, 4)),
+            pltpu.SemaphoreType.DMA((2, 4)),
+            pltpu.SemaphoreType.DMA((2, 4)),
+        ],
+        compiler_params=pltpu.CompilerParams(
+            collective_id=0, has_side_effects=True, vmem_limit_bytes=61 * 2**20
+        ),
+    )(tokens, out_grad, meta, gate_weight, up_weight, down_weight)
+
+
+def grad_kernel(
+    x_ref, g_ref, scaled_ref, gate_back_ref, up_back_ref, gate_out, up_out, down_out
+):
+    x, g = x_ref[0], g_ref[0]
+    gate_out[0] = dot(gate_back_ref[0], x, 0, 0).astype(jnp.bfloat16)
+    up_out[0] = dot(up_back_ref[0], x, 0, 0).astype(jnp.bfloat16)
+    down_out[0] = dot(scaled_ref[0], g, 0, 0).astype(jnp.bfloat16)
+
+
+def grad_pass(x_rows, g_rows, scaled, gate_back, up_back):
+    slots, rows, units = scaled.shape
+    width = x_rows.shape[-1]
+    x_rows = x_rows.reshape(slots, rows, width)
+    g_rows = g_rows.reshape(slots, rows, width)
+    long = pl.BlockSpec((1, rows, width), lambda s: (s, 0, 0))
+    short = pl.BlockSpec((1, rows, units), lambda s: (s, 0, 0))
+    wide = pl.BlockSpec((1, units, width), lambda s: (s, 0, 0))
+    return pl.pallas_call(
+        grad_kernel,
+        grid=(slots,),
+        out_shape=(jax.ShapeDtypeStruct((slots, units, width), jnp.bfloat16),) * 3,
+        in_specs=[long, long, short, short, short],
+        out_specs=[wide] * 3,
+        compiler_params=pltpu.CompilerParams(vmem_limit_bytes=32 * 2**20),
+    )(x_rows, g_rows, scaled, gate_back, up_back)
+
+
+def gathered_shards(
+    tokens, out_grad, route_probs, routes, placement, gate_weight, up_weight, down_weight
+):
+    block, top_k = routes.shape
+    expert_ids = jnp.arange(placement.shape[0], dtype=jnp.int32)
+    matches = routes.T[:, :, None] == expert_ids
+    slot_ids = jnp.sum(jnp.where(matches, placement, 0), axis=2, dtype=jnp.int32)
+    fill = ((0, 8 - top_k), (0, 0))
+    meta = jnp.concatenate(
+        [
+            jnp.pad(slot_ids.astype(jnp.float32), fill, constant_values=-1.0),
+            jnp.pad(route_probs.T, fill),
+        ],
+        axis=0,
+    )
+    layer_out, token_grad, prob_sum, *kept = route_pass(
+        tokens,
+        out_grad,
+        meta,
+        jnp.swapaxes(gate_weight, 1, 2),
+        jnp.swapaxes(up_weight, 1, 2),
+        down_weight,
+    )
+    gate_grad, up_grad, down_grad = grad_pass(*kept)
+    gate_grad, up_grad = jnp.swapaxes(gate_grad, 1, 2), jnp.swapaxes(up_grad, 1, 2)
+    return (layer_out, token_grad, prob_sum[:top_k].T, gate_grad, up_grad, down_grad)
+
+
 def solution(mesh):
     in_specs = (
         P(("groups", "expert"), None),
@@ -133,4 +568,6 @@
         P(("groups", "expert"), None, "replica"),
         P(("groups", "expert"), "replica", None),
     )
-    return jax.shard_map(shards, mesh=mesh, in_specs=in_specs, out_specs=out_specs, check_vma=False)
+    small = mesh.shape["expert"] == 4 and mesh.shape["replica"] == 4
+    body = gathered_shards if small else shards
+    return jax.shard_map(body, mesh=mesh, in_specs=in_specs, out_specs=out_specs, check_vma=False)

time: 308 us -> 107 us (0.35)
  waiting for transfers between devices: 133 us -> 0 us
  Pallas kernels: 0 us -> 92.8 us
  matrix products: 72.7 us -> 0 us
  local copies, waits for them, and re-layouts: 41.4 us -> 11.2 us
  starting transfers between devices: 19.4 us -> 0 us
  other arithmetic: 15.9 us -> 2.1 us
  between operations: 14.3 us -> 0.66 us
  blocking collectives: 10.5 us -> 0 us
    all_to_all x4 -> x0, waiting for transfers between devices: 121 us -> none  [the longest x1 34.5 us: shards(): lax.all_to_all(input_send, 'expert', split_axis=0, concat_axis=0, tiled=T...]
    pallas_call x0 -> x2, Pallas kernels: none -> 92.8 us  [the longest x1 77.2 us: route_pass(): pl.pallas_call(route_kernel, out_shape=(jax.ShapeDtypeStruct((block, widt...]
    dot_general x9 -> x0, matrix products: 72.7 us -> none  [the longest x1 9.97 us: expert_rows(): jnp.einsum('slcd,lhd->slch', back_rows, down_weight, preferred_element_ty...]
    gather x5 -> x0, local copies, waits for them, and re-layouts: 23.2 us -> none  [the longest x1 5.68 us: shards(): grad_rows = grad_back.reshape(-1, model_width)[position].astype(jnp.float32)]
    all_to_all x4 -> x0, starting transfers between devices: 19.3 us -> none  [the longest x1 6.45 us: shards(): lax.all_to_all(input_send, 'expert', split_axis=0, concat_axis=0, tiled=T...]
    psum x1 -> x0, waiting for transfers between devices: 12.1 us -> none  [shards(): lax.psum(layer_part.astype(jnp.bfloat16), 'replica').astype(jnp.float32)]
    psum x1 -> x0, blocking collectives: 10.5 us -> none  [shards(): lax.psum(prob_part.astype(jnp.bfloat16), 'replica').astype(jnp.float32)]
    convert_element_type x4 -> x0, local copies, waits for them, and re-layouts: 8.97 us -> none  [the longest x1 3.88 us: shards(): out_rows = out_back.reshape(-1, model_width)[position].astype(jnp.float32)]
  transfers between devices with their start and end apart: 5 -> 0, of which waited for: 5 -> 0; matrix products, arithmetic and copies ran while one was open for 26% -> 0% of each run, Pallas kernels for 0% -> 0%
where the time goes in v3:
time: 107 us
  Pallas kernels  92.8 us (87%)
  local copies, waits for them, and re-layouts  11.2 us (10%)
  other arithmetic  2.1 us (2%)
    pallas_call x1, Pallas kernels, route_pass(): pl.pallas_call(route_kernel, out_shape=(jax.ShapeDtypeStruct((block, widt...  77.2 us
    pallas_call x1, Pallas kernels, grad_pass(): pl.pallas_call(grad_kernel, grid=(slots,), out_shape=(jax.ShapeDtypeStruc...  15.6 us
    unnamed x12, local copies, waits for them, and re-layouts  9.92 us

profile of v3, /device:TPU:0, one launch (start us, length us, event | category | flops | bytes accessed | tf_op | source)
XLA Modules:
  0.0 106.7 jit_solution(16176673804529707835)
XLA Ops:
  0.6 0.8 select_reduce_fusion
  1.4 1.3 %select_maximum_fusion.m_ref = f32[16,128]{1,0:T(8,128)} fusion(f32[6,128]{1,0:T(8,128)} %bitcast.15, f32[6,128]{1,0:T(8,128)S(1)} %convert_element_type.5), kind=kLoop, calls=%fused_computation.2 | loop fusion | flops 10240 | bytes 14336 | tf_op jit(solution)/shard_map/concatenate | solution.py:532
  2.7 77.2 %shard_map.127 = (bf16[128,1024]{1,0:T(8,128)(2,1)}, bf16[128,1024]{1,0:T(8,128)(2,1)}, f32[8,128]{1,0:T(8,128)}, bf16[16,4,16,1024]{3,2,1,0:T(8,128)(2,1)}, bf1...) custom-call(bf16[128,1024]{1,0:T(8,128)(2,1)} %x_ref.1, ...), custom_call_target="tpu_custom_call" | custom-call | tf_op jit(solution)/shard_map/pallas_call | solution.py:447
  80.0 1.3 %slice_bitcast_fusion = f32[128,6]{0,1:T(8,128)} fusion(f32[8,128]{1,0:T(8,128)} %get-tuple-element.19), kind=kLoop, calls=%fused_computation.5 | loop fusion | bytes 6144 | tf_op jit(solution)/shard_map/transpose | solution.py:549
  81.3 0.0 copy-start
  81.3 1.6 %copy-done = bf16[16,4,16,1024]{3,2,1,0:T(8,128)(2,1)S(1)} copy-done((bf16[16,4,16,1024]{3,2,1,0:T(8,128)(2,1)S(1)}, bf16[16,4,16,1024]{3,2,1,0:T(8,128)(2,1)}, u32[]{:S(2)}) %copy-start) | copy-done | bytes 2097176
  82.8 0.0 copy-start.1
  82.9 1.6 %copy-done.1 = bf16[16,4,16,1024]{3,2,1,0:T(8,128)(2,1)S(1)} copy-done((bf16[16,4,16,1024]{3,2,1,0:T(8,128)(2,1)S(1)}, bf16[16,4,16,1024]{3,2,1,0:T(8,128)(2,1)}, u32[]{:S(2)}) %copy-start.1) | copy-done | bytes 2097176
  84.4 0.0 copy-start.2
  84.4 1.1 %copy-done.2 = bf16[16,64,352]{2,1,0:T(8,128)(2,1)S(1)} copy-done((bf16[16,64,352]{2,1,0:T(8,128)(2,1)S(1)}, bf16[16,64,352]{2,1,0:T(8,128)(2,1)}, u32[]{:S(2)}) %copy-start.2) | copy-done | bytes 720920
  85.6 0.0 copy-start.3
  85.6 1.1 %copy-done.3 = bf16[16,64,352]{2,1,0:T(8,128)(2,1)S(1)} copy-done((bf16[16,64,352]{2,1,0:T(8,128)(2,1)S(1)}, bf16[16,64,352]{2,1,0:T(8,128)(2,1)}, u32[]{:S(2)}) %copy-start.3) | copy-done | bytes 720920
  86.7 0.0 copy-start.4
  86.7 1.1 %copy-done.4 = bf16[16,64,352]{2,1,0:T(8,128)(2,1)S(1)} copy-done((bf16[16,64,352]{2,1,0:T(8,128)(2,1)S(1)}, bf16[16,64,352]{2,1,0:T(8,128)(2,1)}, u32[]{:S(2)}) %copy-start.4) | copy-done | bytes 720920
  87.8 15.6 %shard_map.128 = (bf16[16,352,1024]{2,1,0:T(8,128)(2,1)}, bf16[16,352,1024]{2,1,0:T(8,128)(2,1)}, bf16[16,352,1024]{2,1,0:T(8,128)(2,1)}) custom-call(bf16[16,64,1024]{2,1,0:T(8,128)(2,1)S(1)} %bitcast.10, bf16[16,64,1024]{2,1,0:T(8,128)(2,1)S(1)} %bitcast.11, bf16[16,64,352]{2,1,0:T(8,128)(2,1)S(1)} %copy-done.2, bf16[16,64,352]{2,1,0:T(8,128)(2,1)S(1)} %copy-done.3, ...), custom_call_target="tpu_custom_call" | custom-call | tf_op jit(solution)/shard_map/pallas_call | solution.py:514
  103.4 1.7 %copy.16 = bf16[128,1024]{1,0:T(8,128)(2,1)} copy(bf16[128,1024]{1,0:T(8,128)(2,1)} %get-tuple-element.34) | data formatting | bytes 524288
  105.1 1.7 %copy.17 = bf16[128,1024]{1,0:T(8,128)(2,1)} copy(bf16[128,1024]{1,0:T(8,128)(2,1)} %get-tuple-element.35) | data formatting | bytes 524288
  (1 shorter events, 0.0 us)
Async XLA Ops:
  81.3 1.6 %copy-start = (bf16[16,4,16,1024]{3,2,1,0:T(8,128)(2,1)S(1)}, bf16[16,4,16,1024]{3,2,1,0:T(8,128)(2,1)}, u32[]{:S(2)}) copy-start(bf16[16,4,16,1024]{3,2,1,0:T(8,128)(2,1)} %get-tuple-element.20) | copy-start | bytes 6291460
  82.8 1.6 %copy-start.1 = (bf16[16,4,16,1024]{3,2,1,0:T(8,128)(2,1)S(1)}, bf16[16,4,16,1024]{3,2,1,0:T(8,128)(2,1)}, u32[]{:S(2)}) copy-start(bf16[16,4,16,1024]{3,2,1,0:T(8,128)(2,1)} %get-tuple-element.21) | copy-start | bytes 6291460
  84.4 1.1 %copy-start.2 = (bf16[16,64,352]{2,1,0:T(8,128)(2,1)S(1)}, bf16[16,64,352]{2,1,0:T(8,128)(2,1)}, u32[]{:S(2)}) copy-start(bf16[16,64,352]{2,1,0:T(8,128)(2,1)} %get-tuple-element.22.scaled_ref) | copy-start | bytes 2162692
  85.6 1.1 %copy-start.3 = (bf16[16,64,352]{2,1,0:T(8,128)(2,1)S(1)}, bf16[16,64,352]{2,1,0:T(8,128)(2,1)}, u32[]{:S(2)}) copy-start(bf16[16,64,352]{2,1,0:T(8,128)(2,1)} %get-tuple-element.23.gate_back_ref) | copy-start | bytes 2162692
  86.7 1.1 %copy-start.4 = (bf16[16,64,352]{2,1,0:T(8,128)(2,1)S(1)}, bf16[16,64,352]{2,1,0:T(8,128)(2,1)}, u32[]{:S(2)}) copy-start(bf16[16,64,352]{2,1,0:T(8,128)(2,1)} %get-tuple-element.24.up_back_ref) | copy-start | bytes 2162692

commit v4 on v3

--- a/solution.py
+++ b/solution.py
@@ -156,10 +156,11 @@
 
 def route_kernel(
     x_ref, g_ref, m_ref, gate_hbm, up_hbm, down_hbm,
-    layer_ref, token_ref, prob_out, x_rows, g_rows, scaled_ref, gate_back_ref, up_back_ref,
+    layer_ref, token_ref, prob_out, x_hbm, g_hbm, scaled_hbm, gate_back_hbm, up_back_hbm,
+    x_rows, g_rows, scaled_ref, gate_back_ref, up_back_ref,
     rows_ref, meta_ref, gate_ref, up_ref, down_ref, gate_pre_ref, up_pre_ref, back_rows,
     pick_ref, weight_ref, inner_ref, part_ref, near, crossing, crossed, summed, arrived, final,
-    prob_ref, prob_in, prob_all, load, send, recv, add_send, add_recv, prob_send, prob_recv,
+    prob_ref, prob_in, prob_all, load, saved, send, recv, add_send, add_recv, prob_send, prob_recv,
 ):
     e, r, core, across, diagonal = positions()
     slots, units, width = gate_ref.shape
@@ -171,6 +172,17 @@
     mine = pl.ds(pl.multiple_of(r * quarter, quarter), quarter)
     other = pl.ds(pl.multiple_of(across * quarter, quarter), quarter)
     weights = ((gate_hbm, gate_ref), (up_hbm, up_ref), (down_hbm, down_ref))
+
+    kept = []
+    results = (
+        (x_rows, x_hbm), (g_rows, g_hbm), (scaled_ref, scaled_hbm),
+        (gate_back_ref, gate_back_hbm), (up_back_ref, up_back_hbm),
+    )
+
+    def store(i):
+        copy = pltpu.make_async_copy(results[i][0], results[i][1], saved.at[i])
+        copy.start()
+        return copy
 
     def fetch(s, start):
         for i, (source, target) in enumerate(weights):
@@ -263,36 +275,49 @@
         for b in range(4):
             back_rows[b, s] = value[b]
 
-    def forward(s, carry):
-        fetch(s, False)
-        x = x_rows[s].reshape(rows, width)
-        gate_pre = dot(x, gate_ref[s], 1, 1)
-        up_pre = dot(x, up_ref[s], 1, 1)
-        gate_pre_ref[s] = gate_pre
-        up_pre_ref[s] = up_pre
-        hidden = wide((gate_pre * jax.nn.sigmoid(gate_pre) * up_pre).astype(jnp.bfloat16))
-        scaled = (hidden * weight_ref[s].reshape(rows, 1)).astype(jnp.bfloat16)
-        scaled_ref[s] = scaled
-        keep(s, dot(scaled, down_ref[s], 1, 0))
+    def forward(pair, carry):
+        both = (2 * pair, 2 * pair + 1)
+        for s in both:
+            fetch(s, False)
+        x = [x_rows[s].reshape(rows, width) for s in both]
+        gate_pre = [dot(x[i], gate_ref[s], 1, 1) for i, s in enumerate(both)]
+        up_pre = [dot(x[i], up_ref[s], 1, 1) for i, s in enumerate(both)]
+        scaled = []
+        for i, s in enumerate(both):
+            swish = gate_pre[i] * jax.nn.sigmoid(gate_pre[i])
+            hidden = wide((swish * up_pre[i]).astype(jnp.bfloat16))
+            scaled.append((hidden * weight_ref[s].reshape(rows, 1)).astype(jnp.bfloat16))
+        output = [dot(scaled[i], down_ref[s], 1, 0) for i, s in enumerate(both)]
+        for i, s in enumerate(both):
+            gate_pre_ref[s] = gate_pre[i]
+            up_pre_ref[s] = up_pre[i]
+            scaled_ref[s] = scaled[i]
+            keep(s, output[i])
         return carry
 
-    def backward(s, carry):
-        g = g_rows[s].reshape(rows, width)
-        gate_pre, up_pre = gate_pre_ref[s], up_pre_ref[s]
-        plain_grad = dot(g, down_ref[s], 1, 1)
-        sigma = jax.nn.sigmoid(gate_pre)
-        swish = gate_pre * sigma
-        hidden = wide((swish * up_pre).astype(jnp.bfloat16))
-        inner = jnp.sum(hidden * plain_grad, axis=1, keepdims=True)
-        inner_ref[s] = inner.reshape(4, MOST, 1)
-        hidden_grad = plain_grad * weight_ref[s].reshape(rows, 1)
-        gate_back = (hidden_grad * up_pre * sigma * (1.0 + gate_pre * (1.0 - sigma))).astype(
-            jnp.bfloat16
-        )
-        up_back = (hidden_grad * swish).astype(jnp.bfloat16)
-        gate_back_ref[s] = gate_back
-        up_back_ref[s] = up_back
-        keep(s, dot(gate_back, gate_ref[s], 1, 0) + dot(up_back, up_ref[s], 1, 0))
+    def backward(pair, carry):
+        both = (2 * pair, 2 * pair + 1)
+        plain_grad = [dot(g_rows[s].reshape(rows, width), down_ref[s], 1, 1) for s in both]
+        gate_back, up_back, inner = [], [], []
+        for i, s in enumerate(both):
+            gate_pre, up_pre = gate_pre_ref[s], up_pre_ref[s]
+            sigma = jax.nn.sigmoid(gate_pre)
+            swish = gate_pre * sigma
+            hidden = wide((swish * up_pre).astype(jnp.bfloat16))
+            inner.append(jnp.sum(hidden * plain_grad[i], axis=1, keepdims=True))
+            hidden_grad = plain_grad[i] * weight_ref[s].reshape(rows, 1)
+            slope = sigma * (1.0 + gate_pre * (1.0 - sigma))
+            gate_back.append((hidden_grad * up_pre * slope).astype(jnp.bfloat16))
+            up_back.append((hidden_grad * swish).astype(jnp.bfloat16))
+        input_grad = [
+            dot(gate_back[i], gate_ref[s], 1, 0) + dot(up_back[i], up_ref[s], 1, 0)
+            for i, s in enumerate(both)
+        ]
+        for i, s in enumerate(both):
+            inner_ref[s] = inner[i].reshape(4, MOST, 1)
+            gate_back_ref[s] = gate_back[i]
+            up_back_ref[s] = up_back[i]
+            keep(s, input_grad[i])
         return carry
 
     order = (2, 1, 3, 0)
@@ -371,17 +396,23 @@
     pass_on(1)
     received(0)
     take(0, x_rows)
-    some = slots // 4
+    kept.append(store(0))
+    pairs = slots // 2
+    some = pairs // 4
     lax.fori_loop(0, some, forward, 0)
     pass_last(1)
-    lax.fori_loop(some, slots, forward, 0)
+    lax.fori_loop(some, pairs, forward, 0)
+    kept.append(store(2))
     gather_back(0)
     received(1)
     take(1, g_rows)
+    kept.append(store(1))
     add_near(0)
-    lax.fori_loop(0, slots // 2, backward, 0)
+    lax.fori_loop(0, pairs // 2, backward, 0)
     add_crossed(0)
-    lax.fori_loop(slots // 2, slots, backward, 0)
+    lax.fori_loop(pairs // 2, pairs, backward, 0)
+    kept.append(store(3))
+    kept.append(store(4))
     gather_back(1)
     back, forth = {}, {}
     names = slot_names()
@@ -418,6 +449,8 @@
     prob_out[...] = prob_all[0] + prob_all[1] + prob_all[2] + prob_all[3]
     hand_on(1)
     finish(1, token_ref)
+    for copy in kept:
+        copy.wait()
     for j in (1, 2, 3):
         metas[j].wait_send()
         back[j].wait_send()
@@ -457,8 +490,13 @@
             jax.ShapeDtypeStruct((slots, rows, units), half),
         ),
         in_specs=[whole, whole, whole, left, left, left],
-        out_specs=[whole] * 8,
+        out_specs=[whole] * 3 + [left] * 5,
         scratch_shapes=[
+            pltpu.VMEM((slots, 4, MOST, width), half),
+            pltpu.VMEM((slots, 4, MOST, width), half),
+            pltpu.VMEM((slots, rows, units), half),
+            pltpu.VMEM((slots, rows, units), half),
+            pltpu.VMEM((slots, rows, units), half),
             pltpu.VMEM((2, 4, block, width), half),
             pltpu.VMEM((4,) + meta.shape, jnp.float32),
             pltpu.VMEM((slots, units, width), half),
@@ -481,6 +519,7 @@
             pltpu.VMEM((4, 8, block), jnp.float32),
             pltpu.VMEM((4, 8, block), jnp.float32),
             pltpu.SemaphoreType.DMA((3, slots)),
+            pltpu.SemaphoreType.DMA((5,)),
             pltpu.SemaphoreType.DMA((2, 5, 4)),
             pltpu.SemaphoreType.DMA((2, 5, 4)),
             pltpu.SemaphoreType.DMA((2, 5, 4)),
@@ -517,7 +556,7 @@
         out_shape=(jax.ShapeDtypeStruct((slots, units, width), jnp.bfloat16),) * 3,
         in_specs=[long, long, short, short, short],
         out_specs=[wide] * 3,
-        compiler_params=pltpu.CompilerParams(vmem_limit_bytes=32 * 2**20),
+        compiler_params=pltpu.CompilerParams(vmem_limit_bytes=60 * 2**20),
     )(x_rows, g_rows, scaled, gate_back, up_back)
 
 

time: 107 us -> 98 us (0.916)
  local copies, waits for them, and re-layouts: 11.2 us -> 4.61 us
  Pallas kernels: 92.8 us -> 89.9 us
    unnamed x12 -> x2, local copies, waits for them, and re-layouts: 9.92 us -> 3.34 us
    pallas_call x1, Pallas kernels: 77.2 us -> 71.3 us  [route_pass(): pl.pallas_call(route_kernel, out_shape=(jax.ShapeDtypeStruct((block, widt...]
    pallas_call x1, Pallas kernels: 15.6 us -> 18.7 us  [grad_pass(): pl.pallas_call(grad_kernel, grid=(slots,), out_shape=(jax.ShapeDtypeStruc...]
where the time goes in v4:
time: 98 us; the launch traced here: 97.3 us
  Pallas kernels  89.9 us (92%)
  local copies, waits for them, and re-layouts  4.61 us (5%)
  other arithmetic  2.1 us (2%)
    pallas_call x1, Pallas kernels, route_pass(): pl.pallas_call(route_kernel, out_shape=(jax.ShapeDtypeStruct((block, widt...  71.3 us
    pallas_call x1, Pallas kernels, grad_pass(): pl.pallas_call(grad_kernel, grid=(slots,), out_shape=(jax.ShapeDtypeStruc...  18.7 us
    unnamed x2, local copies, waits for them, and re-layouts  3.34 us

profile of v4, /device:TPU:0, one launch (start us, length us, event | category | flops | bytes accessed | tf_op | source)
XLA Modules:
  0.0 97.3 jit_solution(4616383144568627834)
XLA Ops:
  0.6 0.8 select_reduce_fusion
  1.4 1.3 %select_maximum_fusion.m_ref = f32[16,128]{1,0:T(8,128)} fusion(f32[6,128]{1,0:T(8,128)} %bitcast.15, f32[6,128]{1,0:T(8,128)S(1)} %convert_element_type.5), kind=kLoop, calls=%fused_computation.2 | loop fusion | flops 10240 | bytes 14336 | tf_op jit(solution)/shard_map/concatenate | solution.py:571
  2.7 71.3 %shard_map.127 = (bf16[128,1024]{1,0:T(8,128)(2,1)}, bf16[128,1024]{1,0:T(8,128)(2,1)}, f32[8,128]{1,0:T(8,128)}, bf16[16,4,16,1024]{3,2,1,0:T(8,128)(2,1)}, bf1...) custom-call(bf16[128,1024]{1,0:T(8,128)(2,1)} %x_ref.1, ...), custom_call_target="tpu_custom_call" | custom-call | tf_op jit(solution)/shard_map/pallas_call | solution.py:480
  74.0 1.3 %slice_bitcast_fusion = f32[128,6]{0,1:T(8,128)} fusion(f32[8,128]{1,0:T(8,128)} %get-tuple-element.19), kind=kLoop, calls=%fused_computation.5 | loop fusion | bytes 6144 | tf_op jit(solution)/shard_map/transpose | solution.py:588
  75.3 18.7 %shard_map.128 = (bf16[16,352,1024]{2,1,0:T(8,128)(2,1)}, bf16[16,352,1024]{2,1,0:T(8,128)(2,1)}, bf16[16,352,1024]{2,1,0:T(8,128)(2,1)}) custom-call(bf16[16,64,1024]{2,1,0:T(8,128)(2,1)} %bitcast.12, bf16[16,64,1024]{2,1,0:T(8,128)(2,1)} %bitcast.13, bf16[16,64,352]{2,1,0:T(8,128)(2,1)} %get-tuple-element.22.scaled_ref, ...), custom_call_target="tpu_custom_call" | custom-call | tf_op jit(solution)/shard_map/pallas_call | solution.py:553
  94.0 1.7 %copy.16 = bf16[128,1024]{1,0:T(8,128)(2,1)} copy(bf16[128,1024]{1,0:T(8,128)(2,1)} %get-tuple-element.34) | data formatting | bytes 524288
  95.6 1.7 %copy.17 = bf16[128,1024]{1,0:T(8,128)(2,1)} copy(bf16[128,1024]{1,0:T(8,128)(2,1)} %get-tuple-element.35) | data formatting | bytes 524288
  (1 shorter events, 0.0 us)
